TPU v7x, 32 devices: a whole 2x2x4 slice. The times are simulated.
32 devices in a mesh: dp: 8 (over y, x, core), tensor: 4 (over z).
Axes of the slice: x: 2, y: 2, z: 4, core: 2. Of those that a mesh axis runs over, the one named last changes fastest.
Arguments:
- inputs: bfloat16 [2, 8, 1024, 2048], P(None, 'dp', 'tensor'), may hold values from -8 to 8
- w_query: bfloat16 [1, 2048, 2048], P(None, 'dp', 'tensor'), may hold values from -0.125 to 0.125
- w_key: bfloat16 [1, 2048, 2048], P(None, 'dp', 'tensor'), may hold values from -0.125 to 0.125
- w_value: bfloat16 [1, 2048, 3456], P(None, 'dp', 'tensor'), may hold values from -0.125 to 0.125
- w_gate: bfloat16 [1, 2048, 3456], P(None, 'dp', 'tensor'), may hold values from -0.125 to 0.125
- w_out: bfloat16 [1, 3456, 2048], P(None, 'tensor', 'dp'), may hold values from -0.109375 to 0.109375
- w_act: bfloat16 [1, 2048, 3456], P(None, 'dp', 'tensor'), may hold values from -0.125 to 0.125
- w_lin: bfloat16 [1, 2048, 3456], P(None, 'dp', 'tensor'), may hold values from -0.125 to 0.125
- w_down: bfloat16 [1, 3456, 2048], P(None, 'tensor', 'dp'), may hold values from -0.109375 to 0.109375
- gain_mix: bfloat16 [1, 2048], P(None, 'dp'), may hold values from 0.25 to 1.75
- gain_ffn: bfloat16 [1, 2048], P(None, 'dp'), may hold values from 0.25 to 1.75
- cotangent: bfloat16 [2, 8, 1024, 2048], P(None, 'dp', 'tensor'), may hold values from -8 to 8
Outputs:
- output: bfloat16 [2, 8, 1024, 2048], P(None, 'dp', 'tensor')
- grad_input: float32 [2, 8, 1024, 2048], P(None, 'dp', 'tensor')
- grad_query: float32 [1, 2048, 2048], P(None, 'dp', 'tensor')
- grad_key: float32 [1, 2048, 2048], P(None, 'dp', 'tensor')
- grad_value: float32 [1, 2048, 3456], P(None, 'dp', 'tensor')
- grad_gate: float32 [1, 2048, 3456], P(None, 'dp', 'tensor')
- grad_out: float32 [1, 3456, 2048], P(None, 'tensor', 'dp')
- grad_act: float32 [1, 2048, 3456], P(None, 'dp', 'tensor')
- grad_lin: float32 [1, 2048, 3456], P(None, 'dp', 'tensor')
- grad_down: float32 [1, 3456, 2048], P(None, 'tensor', 'dp')
- grad_gain_mix: float32 [1, 2048], P(None, 'dp')
- grad_gain_ffn: float32 [1, 2048], P(None, 'dp')
All inputs are finite; a program needn't handle non-finite values.
Results may differ from a plain program's by a relative error of at most 0.02.
Values may be sent and summed in bfloat16 or wider, within the bound.
No kernel may reach another device: no remote copies, remote signals or barrier semaphores. Data moves between devices by JAX's collectives and lax.ppermute only.
A program may use at most 256 MiB of HBM per device.

v0:
```python
import jax
import jax.numpy as jnp
from jax import lax
from jax.sharding import PartitionSpec as P

DK = 256
SEQ = 1024


eps_norm = 1e-06
group_eps = 1.0


def decay_table(head_count, first_head, length, key_size):
    head_ids = (first_head + jnp.arange(head_count, dtype=jnp.int32)).astype(jnp.float32)
    log_rates = jnp.log(1.0 - jnp.exp2(-5.0 - head_ids))
    positions = jnp.arange(length, dtype=jnp.int32)
    offsets = (positions[:, None] - positions[None, :]).astype(jnp.float32)
    causal = offsets >= 0.0
    powers = jnp.exp(jnp.where(causal, offsets, 0.0)[None] * log_rates[:, None, None])
    return jnp.where(causal[None], powers, 0.0) * key_size ** (-0.5)


def rms_inverse(stream, eps_value):
    return lax.rsqrt(jnp.mean(stream * stream, axis=-1, keepdims=True) + eps_value)


def spread_rows(normed_rows):
    return lax.all_gather(normed_rows, "tensor", axis=1, tiled=True)


def collect_rows(partial_value):
    return lax.psum_scatter(
        partial_value.astype(jnp.bfloat16), "tensor", scatter_dimension=1, tiled=True
    ).astype(jnp.float32)


def spread_grads(grad_rows):
    return lax.all_gather(grad_rows, "tensor", axis=1, tiled=True)


def collect_grads(partial_value):
    return lax.psum_scatter(
        partial_value.astype(jnp.bfloat16), "tensor", scatter_dimension=1, tiled=True
    ).astype(jnp.float32)


def fetch_layer(weight_set, layer_id):
    return (
        lax.all_gather(weight_set[0][layer_id], "dp", axis=0, tiled=True),
        lax.all_gather(weight_set[1][layer_id], "dp", axis=0, tiled=True),
        lax.all_gather(weight_set[2][layer_id], "dp", axis=0, tiled=True),
        lax.all_gather(weight_set[3][layer_id], "dp", axis=0, tiled=True),
        lax.all_gather(weight_set[4][layer_id], "dp", axis=1, tiled=True),
        lax.all_gather(weight_set[5][layer_id], "dp", axis=0, tiled=True),
        lax.all_gather(weight_set[6][layer_id], "dp", axis=0, tiled=True),
        lax.all_gather(weight_set[7][layer_id], "dp", axis=1, tiled=True),
        lax.all_gather(weight_set[8][layer_id], "dp", axis=0, tiled=True),
        lax.all_gather(weight_set[9][layer_id], "dp", axis=0, tiled=True),
    )


def project(in_rows, weight_mat):
    return jnp.einsum("bsd,de->bse", in_rows, weight_mat, preferred_element_type=jnp.float32)


def project_back(grad_rows, weight_mat):
    return jnp.einsum("bse,de->bsd", grad_rows, weight_mat, preferred_element_type=jnp.float32)


def weight_grad(in_rows, grad_rows):
    return jnp.einsum("bsd,bse->de", in_rows, grad_rows, preferred_element_type=jnp.float32)


def mix_forward(normed_in, layer_w, decays):
    batch_here = normed_in.shape[0]
    length = normed_in.shape[1]
    heads_here = decays.shape[0]
    queries = (
        project(normed_in, layer_w[0])
        .astype(jnp.bfloat16)
        .reshape(batch_here, length, heads_here, -1)
    )
    key_rows = (
        project(normed_in, layer_w[1])
        .astype(jnp.bfloat16)
        .reshape(batch_here, length, heads_here, -1)
    )
    values = (
        project(normed_in, layer_w[2])
        .astype(jnp.bfloat16)
        .reshape(batch_here, length, heads_here, -1)
    )
    gate_pre = project(normed_in, layer_w[3]).reshape(batch_here, length, heads_here, -1)
    scores = jnp.einsum("bnhk,bmhk->bhnm", queries, key_rows, preferred_element_type=jnp.float32)
    weights_mix = (scores * decays[None]).astype(jnp.bfloat16)
    retained = jnp.einsum(
        "bhnm,bmhv->bnhv", weights_mix, values, preferred_element_type=jnp.float32
    )
    inv_scale = rms_inverse(retained, group_eps)
    normed = retained * inv_scale
    merged = (jax.nn.silu(gate_pre) * normed).astype(jnp.bfloat16).reshape(batch_here, length, -1)
    partial_value = project(merged, layer_w[4])
    return (
        partial_value,
        (queries, key_rows, values, gate_pre, weights_mix, inv_scale, normed, merged),
    )


def mix_backward(normed_in, layer_w, decays, kept, grad_rows):
    queries, key_rows, values, gate_pre, weights_mix, inv_scale, normed, merged = kept
    batch_here = normed_in.shape[0]
    length = normed_in.shape[1]
    grad_w_out = weight_grad(merged, grad_rows)
    merged_grad = jnp.einsum(
        "bsd,ed->bse", grad_rows, layer_w[4], preferred_element_type=jnp.float32
    ).reshape(normed.shape)
    swish, swish_back = jax.vjp(jax.nn.silu, gate_pre)
    gate_grad = (
        swish_back(merged_grad * normed)[0].astype(jnp.bfloat16).reshape(batch_here, length, -1)
    )
    normed_grad = merged_grad * swish
    retained_grad = (
        inv_scale * (normed_grad - normed * jnp.mean(normed_grad * normed, axis=-1, keepdims=True))
    ).astype(jnp.bfloat16)
    mix_grad = jnp.einsum(
        "bnhv,bmhv->bhnm", retained_grad, values, preferred_element_type=jnp.float32
    )
    values_grad = (
        jnp.einsum(
            "bhnm,bnhv->bmhv", weights_mix, retained_grad, preferred_element_type=jnp.float32
        )
        .astype(jnp.bfloat16)
        .reshape(batch_here, length, -1)
    )
    score_grad = (mix_grad * decays[None]).astype(jnp.bfloat16)
    queries_grad = (
        jnp.einsum("bhnm,bmhk->bnhk", score_grad, key_rows, preferred_element_type=jnp.float32)
        .astype(jnp.bfloat16)
        .reshape(batch_here, length, -1)
    )
    keys_grad = (
        jnp.einsum("bhnm,bnhk->bmhk", score_grad, queries, preferred_element_type=jnp.float32)
        .astype(jnp.bfloat16)
        .reshape(batch_here, length, -1)
    )
    grads = (
        weight_grad(normed_in, queries_grad),
        weight_grad(normed_in, keys_grad),
        weight_grad(normed_in, values_grad),
        weight_grad(normed_in, gate_grad),
        grad_w_out,
    )
    in_grad = project_back(queries_grad, layer_w[0]) + project_back(keys_grad, layer_w[1])
    in_grad = in_grad + project_back(values_grad, layer_w[2]) + project_back(gate_grad, layer_w[3])
    return (in_grad, grads)


def ffn_forward(normed_mid, layer_w):
    act_pre = project(normed_mid, layer_w[5])
    lin_pre = project(normed_mid, layer_w[6])
    hidden = (jax.nn.gelu(act_pre) * lin_pre).astype(jnp.bfloat16)
    return (project(hidden, layer_w[7]), (act_pre, lin_pre, hidden))


def ffn_backward(normed_mid, layer_w, kept, grad_rows):
    act_pre, lin_pre, hidden = kept
    grad_w_down = weight_grad(hidden, grad_rows)
    grad_hidden = jnp.einsum(
        "bsd,fd->bsf", grad_rows, layer_w[7], preferred_element_type=jnp.float32
    )
    gelu_val, gelu_back = jax.vjp(jax.nn.gelu, act_pre)
    act_grad = gelu_back(grad_hidden * lin_pre)[0].astype(jnp.bfloat16)
    lin_grad = (grad_hidden * gelu_val).astype(jnp.bfloat16)
    in_grad = project_back(act_grad, layer_w[5]) + project_back(lin_grad, layer_w[6])
    return (
        in_grad,
        (weight_grad(normed_mid, act_grad), weight_grad(normed_mid, lin_grad), grad_w_down),
    )


def norm_forward(stream, gain_row):
    return (stream * rms_inverse(stream, eps_norm) * gain_row).astype(jnp.bfloat16)


def norm_backward(stream, gain_row, grad_norm):
    inv_scale = rms_inverse(stream, eps_norm)
    unit_rows = stream * inv_scale
    grad_gain = jnp.sum(grad_norm * unit_rows, axis=(0, 1))
    grad_unit = grad_norm * gain_row
    grad_stream = inv_scale * (
        grad_unit - unit_rows * jnp.mean(grad_unit * unit_rows, axis=-1, keepdims=True)
    )
    return (grad_stream, grad_gain)


def shards(
    inputs,
    w_query,
    w_key,
    w_value,
    w_gate,
    w_out,
    w_act,
    w_lin,
    w_down,
    gain_mix,
    gain_ffn,
    cotangent,
):
    weight_set = (w_query, w_key, w_value, w_gate, w_out, w_act, w_lin, w_down, gain_mix, gain_ffn)
    layer_count = w_query.shape[0]
    micro_count = inputs.shape[0]
    heads_here = w_query.shape[2] // DK
    decays = decay_table(heads_here, lax.axis_index("tensor") * heads_here, SEQ, DK)
    streams = [inputs[micro_id].astype(jnp.float32) for micro_id in range(micro_count)]
    layer_id = 0
    layer_records = []
    for micro_id in range(micro_count):
        current = fetch_layer(weight_set, layer_id)
        stream = streams[micro_id]
        normed_in = spread_rows(norm_forward(stream, current[8].astype(jnp.float32)))
        partial_value, mix_kept = mix_forward(normed_in, current, decays)
        middle = stream + collect_rows(partial_value)
        normed_mid = spread_rows(norm_forward(middle, current[9].astype(jnp.float32)))
        partial_value, ffn_kept = ffn_forward(normed_mid, current)
        streams[micro_id] = middle + collect_rows(partial_value)
        layer_records.append((stream, normed_in, mix_kept, middle, normed_mid, ffn_kept))
    records = [layer_records]
    grads_now = [cotangent[micro_id].astype(jnp.float32) for micro_id in range(micro_count)]
    layer_sums = [None] * layer_count
    for layer_id in reversed(range(layer_count)):
        for micro_id in range(micro_count):
            current = fetch_layer(weight_set, layer_id)
            stream, normed_in, mix_kept, middle, normed_mid, ffn_kept = records[layer_id][micro_id]
            grad_stream = grads_now[micro_id]
            grad_rows = spread_grads(grad_stream.astype(jnp.bfloat16))
            in_grad, ffn_grads = ffn_backward(normed_mid, current, ffn_kept, grad_rows)
            grad_mid, gain_second = norm_backward(
                middle, current[9].astype(jnp.float32), collect_grads(in_grad)
            )
            grad_middle = grad_stream + grad_mid
            grad_rows = spread_grads(grad_middle.astype(jnp.bfloat16))
            in_grad, mix_grads = mix_backward(normed_in, current, decays, mix_kept, grad_rows)
            grad_first, gain_first = norm_backward(
                stream, current[8].astype(jnp.float32), collect_grads(in_grad)
            )
            grads_now[micro_id] = grad_middle + grad_first
            terms = mix_grads + ffn_grads + (gain_first, gain_second)
            if micro_id == 0:
                layer_sums[layer_id] = terms
            else:
                layer_sums[layer_id] = jax.tree.map(jnp.add, layer_sums[layer_id], terms)
    stacked = [jnp.stack([layer_sums[0][kind_id]]) for kind_id in range(10)]
    reduced = (
        lax.psum_scatter(
            stacked[0].astype(jnp.bfloat16), "dp", scatter_dimension=1, tiled=True
        ).astype(jnp.float32),
        lax.psum_scatter(
            stacked[1].astype(jnp.bfloat16), "dp", scatter_dimension=1, tiled=True
        ).astype(jnp.float32),
        lax.psum_scatter(
            stacked[2].astype(jnp.bfloat16), "dp", scatter_dimension=1, tiled=True
        ).astype(jnp.float32),
        lax.psum_scatter(
            stacked[3].astype(jnp.bfloat16), "dp", scatter_dimension=1, tiled=True
        ).astype(jnp.float32),
        lax.psum_scatter(
            stacked[4].astype(jnp.bfloat16), "dp", scatter_dimension=2, tiled=True
        ).astype(jnp.float32),
        lax.psum_scatter(
            stacked[5].astype(jnp.bfloat16), "dp", scatter_dimension=1, tiled=True
        ).astype(jnp.float32),
        lax.psum_scatter(
            stacked[6].astype(jnp.bfloat16), "dp", scatter_dimension=1, tiled=True
        ).astype(jnp.float32),
        lax.psum_scatter(
            stacked[7].astype(jnp.bfloat16), "dp", scatter_dimension=2, tiled=True
        ).astype(jnp.float32),
        lax.psum_scatter(
            stacked[8].astype(jnp.bfloat16), "dp", scatter_dimension=1, tiled=True
        ).astype(jnp.float32),
        lax.psum_scatter(
            stacked[9].astype(jnp.bfloat16), "dp", scatter_dimension=1, tiled=True
        ).astype(jnp.float32),
    )
    gain_sums = lax.psum((reduced[8], reduced[9]), "tensor")
    output = jnp.stack(streams).astype(jnp.bfloat16)
    grad_input = jnp.stack(grads_now)
    return (
        output,
        grad_input,
        reduced[0],
        reduced[1],
        reduced[2],
        reduced[3],
        reduced[4],
        reduced[5],
        reduced[6],
        reduced[7],
        gain_sums[0],
        gain_sums[1],
    )


def solution(mesh):
    in_specs = (
        P(None, "dp", "tensor", None),
        P(None, "dp", "tensor"),
        P(None, "dp", "tensor"),
        P(None, "dp", "tensor"),
        P(None, "dp", "tensor"),
        P(None, "tensor", "dp"),
        P(None, "dp", "tensor"),
        P(None, "dp", "tensor"),
        P(None, "tensor", "dp"),
        P(None, "dp"),
        P(None, "dp"),
        P(None, "dp", "tensor", None),
    )
    out_specs = (
        P(None, "dp", "tensor", None),
        P(None, "dp", "tensor", None),
        P(None, "dp", "tensor"),
        P(None, "dp", "tensor"),
        P(None, "dp", "tensor"),
        P(None, "dp", "tensor"),
        P(None, "tensor", "dp"),
        P(None, "dp", "tensor"),
        P(None, "dp", "tensor"),
        P(None, "tensor", "dp"),
        P(None, "dp"),
        P(None, "dp"),
    )
    return jax.shard_map(shards, mesh=mesh, in_specs=in_specs, out_specs=out_specs, check_vma=False)
```

profile of v0, /device:TPU:0, one launch (start us, length us, event | category | flops | bytes accessed | tf_op | source)
XLA Modules:
  0.0 2080.4 jit_solution(502174641482027934)
XLA Ops:
  40.5 82.9 %all-gather.29.cloned.1.call-done = bf16[1,1024,2048]{2,1,0:T(8,128)(2,1)} async-done(((bf16[1,256,2048]{2,1,0:T(8,128)(2,1)}), bf16[1,1024,2048]{2,1,0:T(8,128)(2,1)}) %all-gather.29.cloned.1.call-update) | async-done | bytes 4194320 | tf_op jit(solution)/shard_map/all_gather | solution.py:29
  270.0 73.2 %all-gather.33.cloned.1.call-done = bf16[1,1024,2048]{2,1,0:T(8,128)(2,1)} async-done(((bf16[1,256,2048]{2,1,0:T(8,128)(2,1)}), bf16[1,1024,2048]{2,1,0:T(8,128)(2,1)}) %all-gather.33.cloned.1.call-update) | async-done | bytes 4194320 | tf_op jit(solution)/shard_map/all_gather | solution.py:29
  385.6 35.2 %reduce-scatter.23.cloned.1.call-done = bf16[1,256,2048]{2,1,0:T(8,128)(2,1)} async-done(((bf16[1,1024,2048]{2,1,0:T(8,128)(2,1)}), bf16[1,256,2048]{2,1,0:T(8,128)(2,1)}) %reduce-scatter.23.cloned.1.call-update) | async-done | bytes 1048592 | tf_op jit(solution)/shard_map/reduce_scatter | solution.py:33
  420.7 79.7 %reduce-scatter.27.cloned.1.call-done = bf16[1,256,2048]{2,1,0:T(8,128)(2,1)} async-done(((bf16[1,1024,2048]{2,1,0:T(8,128)(2,1)}), bf16[1,256,2048]{2,1,0:T(8,128)(2,1)}) %reduce-scatter.27.cloned.1.call-update) | async-done | bytes 1048592 | tf_op jit(solution)/shard_map/reduce_scatter | solution.py:33
  511.1 26.1 %all-gather.53.cloned.1.call-done = bf16[1,2048,864]{1,2,0:T(8,128)(2,1)} async-done(((bf16[1,256,864]{1,2,0:T(8,128)(2,1)}), bf16[1,2048,864]{1,2,0:T(8,128)(2,1)}) %all-gather.53.cloned.1.call-update) | async-done | bytes 3538960 | tf_op jit(solution)/shard_map/all_gather | solution.py:56
  537.3 82.9 %all-gather.31.cloned.1.call-done = bf16[1,1024,2048]{2,1,0:T(8,128)(2,1)} async-done(((bf16[1,256,2048]{2,1,0:T(8,128)(2,1)}), bf16[1,1024,2048]{2,1,0:T(8,128)(2,1)}) %all-gather.31.cloned.1.call-update) | async-done | bytes 4194320 | tf_op jit(solution)/shard_map/all_gather | solution.py:29
  664.0 27.5 %all-gather.55.cloned.1.call-done = bf16[1,864,2048]{2,1,0:T(8,128)(2,1)} async-done(((bf16[1,864,256]{2,1,0:T(8,128)(2,1)}), bf16[1,864,2048]{2,1,0:T(8,128)(2,1)}) %all-gather.55.cloned.1.call-update) | async-done | bytes 3538960 | tf_op jit(solution)/shard_map/all_gather | solution.py:57
  691.5 82.2 %all-gather.57.cloned.1.call-done = bf16[1,1,1024,2048]{3,2,1,0:T(8,128)(2,1)} async-done(((bf16[1,1,256,2048]{3,2,1,0:T(8,128)(2,1)}), bf16[1,1,1024,2048]{3,2,1,0:T(8,128)(2,1)}) %all-gather.57.cloned.1.call-update) | async-done | bytes 4194320 | tf_op jit(solution)/shard_map/all_gather | solution.py:39
  797.5 57.0 %all-gather.35.cloned.1.call-done = bf16[1,1024,2048]{2,1,0:T(8,128)(2,1)} async-done(((bf16[1,256,2048]{2,1,0:T(8,128)(2,1)}), bf16[1,1024,2048]{2,1,0:T(8,128)(2,1)}) %all-gather.35.cloned.1.call-update) | async-done | bytes 4194320 | tf_op jit(solution)/shard_map/all_gather | solution.py:29
  869.1 66.1 %all-gather.59.cloned.1.call-done = bf16[1,1,1024,2048]{3,2,1,0:T(8,128)(2,1)} async-done(((bf16[1,1,256,2048]{3,2,1,0:T(8,128)(2,1)}), bf16[1,1,1024,2048]{3,2,1,0:T(8,128)(2,1)}) %all-gather.59.cloned.1.call-update) | async-done | bytes 4194320 | tf_op jit(solution)/shard_map/all_gather | solution.py:39
  967.9 44.8 %reduce-scatter.31.cloned.1.call-done = bf16[1,256,2048]{2,1,0:T(8,128)(2,1)} async-done(((bf16[1,1024,2048]{2,1,0:T(8,128)(2,1)}), bf16[1,256,2048]{2,1,0:T(8,128)(2,1)}) %reduce-scatter.31.cloned.1.call-update) | async-done | bytes 1048592 | tf_op jit(solution)/shard_map/reduce_scatter | solution.py:43
  1012.7 79.6 %reduce-scatter.35.cloned.1.call-done = bf16[1,256,2048]{2,1,0:T(8,128)(2,1)} async-done(((bf16[1,1024,2048]{2,1,0:T(8,128)(2,1)}), bf16[1,256,2048]{2,1,0:T(8,128)(2,1)}) %reduce-scatter.35.cloned.1.call-update) | async-done | bytes 1048592 | tf_op jit(solution)/shard_map/reduce_scatter | solution.py:43
  1095.7 76.2 %reduce-scatter.29.cloned.1.call-done = bf16[1,256,2048]{2,1,0:T(8,128)(2,1)} async-done(((bf16[1,1024,2048]{2,1,0:T(8,128)(2,1)}), bf16[1,256,2048]{2,1,0:T(8,128)(2,1)}) %reduce-scatter.29.cloned.1.call-update) | async-done | bytes 1048592 | tf_op jit(solution)/shard_map/reduce_scatter | solution.py:33
  1215.0 43.5 %all-gather.37.cloned.1.call-done = bf16[1,1024,2048]{2,1,0:T(8,128)(2,1)} async-done(((bf16[1,256,2048]{2,1,0:T(8,128)(2,1)}), bf16[1,1024,2048]{2,1,0:T(8,128)(2,1)}) %all-gather.37.cloned.1.call-update) | async-done | bytes 4194320 | tf_op jit(solution)/shard_map/all_gather | solution.py:39
  1270.3 69.1 %all-gather.39.cloned.1.call-done = bf16[1,1024,2048]{2,1,0:T(8,128)(2,1)} async-done(((bf16[1,256,2048]{2,1,0:T(8,128)(2,1)}), bf16[1,1024,2048]{2,1,0:T(8,128)(2,1)}) %all-gather.39.cloned.1.call-update) | async-done | bytes 4194320 | tf_op jit(solution)/shard_map/all_gather | solution.py:39
  1532.9 43.4 %reduce-scatter.41.cloned.1.call-done = bf16[1,256,512]{2,1,0:T(8,128)(2,1)} async-done(((bf16[1,2048,512]{2,1,0:T(8,128)(2,1)}), bf16[1,256,512]{2,1,0:T(8,128)(2,1)}) %reduce-scatter.41.cloned.1.call-update) | async-done | bytes 262160 | tf_op jit(solution)/shard_map/reduce_scatter | solution.py:259
  1578.2 43.5 %reduce-scatter.39.cloned.1.call-done = bf16[1,256,512]{2,1,0:T(8,128)(2,1)} async-done(((bf16[1,2048,512]{2,1,0:T(8,128)(2,1)}), bf16[1,256,512]{2,1,0:T(8,128)(2,1)}) %reduce-scatter.39.cloned.1.call-update) | async-done | bytes 262160 | tf_op jit(solution)/shard_map/reduce_scatter | solution.py:256
  1623.5 49.8 %reduce-scatter.47.cloned.1.call-done = bf16[1,864,256]{2,1,0:T(8,128)(2,1)} async-done(((bf16[1,864,2048]{2,1,0:T(8,128)(2,1)}), bf16[1,864,256]{2,1,0:T(8,128)(2,1)}) %reduce-scatter.47.cloned.1.call-update) | async-done | bytes 442384 | tf_op jit(solution)/shard_map/reduce_scatter | solution.py:268
  1675.3 49.6 %reduce-scatter.43.cloned.1.call-done = bf16[1,256,864]{1,2,0:T(8,128)(2,1)} async-done(((bf16[1,2048,864]{1,2,0:T(8,128)(2,1)}), bf16[1,256,864]{1,2,0:T(8,128)(2,1)}) %reduce-scatter.43.cloned.1.call-update) | async-done | bytes 442384 | tf_op jit(solution)/shard_map/reduce_scatter | solution.py:262
  1726.9 49.4 %reduce-scatter.45.cloned.1.call-done = bf16[1,256,864]{1,2,0:T(8,128)(2,1)} async-done(((bf16[1,2048,864]{1,2,0:T(8,128)(2,1)}), bf16[1,256,864]{1,2,0:T(8,128)(2,1)}) %reduce-scatter.45.cloned.1.call-update) | async-done | bytes 442384 | tf_op jit(solution)/shard_map/reduce_scatter | solution.py:265
  1778.3 77.7 %reduce-scatter.33.cloned.1.call-done = bf16[1,256,2048]{2,1,0:T(8,128)(2,1)} async-done(((bf16[1,1024,2048]{2,1,0:T(8,128)(2,1)}), bf16[1,256,2048]{2,1,0:T(8,128)(2,1)}) %reduce-scatter.33.cloned.1.call-update) | async-done | bytes 1048592 | tf_op jit(solution)/shard_map/reduce_scatter | solution.py:43
  1856.0 79.7 %reduce-scatter.37.cloned.1.call-done = bf16[1,256,2048]{2,1,0:T(8,128)(2,1)} async-done(((bf16[1,1024,2048]{2,1,0:T(8,128)(2,1)}), bf16[1,256,2048]{2,1,0:T(8,128)(2,1)}) %reduce-scatter.37.cloned.1.call-update) | async-done | bytes 1048592 | tf_op jit(solution)/shard_map/reduce_scatter | solution.py:43
  1944.8 70.3 %reduce-scatter.25.cloned.1.call-done = bf16[1,256,2048]{2,1,0:T(8,128)(2,1)} async-done(((bf16[1,1024,2048]{2,1,0:T(8,128)(2,1)}), bf16[1,256,2048]{2,1,0:T(8,128)(2,1)}) %reduce-scatter.25.cloned.1.call-update) | async-done | bytes 1048592 | tf_op jit(solution)/shard_map/reduce_scatter | solution.py:33
  2022.9 30.2 %reduce-scatter.55.cloned.1.call-done = bf16[256,1]{1,0:T(8,128)(2,1)} async-done(((bf16[2048,1]{1,0:T(8,128)(2,1)}), bf16[256,1]{1,0:T(8,128)(2,1)}) %reduce-scatter.55.cloned.1.call-update) | async-done | bytes 528
  (425 shorter events, 644.7 us)
Async XLA Ops:
  24.4 236.3 %all-gather.49.cloned.1.call-start = ((), (), s32[]{:S(2)}) async-start(), calls=%async_computation.44 | async-start | bytes 3981312 | tf_op jit(solution)/shard_map/all_gather | solution.py:54
  25.0 318.1 %all-gather.33.cloned.1.call-start = ((), (), s32[]{:S(2)}) async-start(), calls=%async_computation.22 | async-start | bytes 5242880 | tf_op jit(solution)/shard_map/all_gather | solution.py:29
  25.8 395.0 %reduce-scatter.23.cloned.1.call-start = ((), (), s32[]{:S(2)}) async-start(), calls=%async_computation.19 | async-start | bytes 5242880 | tf_op jit(solution)/shard_map/reduce_scatter | solution.py:33
  269.9 230.5 %reduce-scatter.27.cloned.1.call-start = ((), (), s32[]{:S(2)}) async-start(), calls=%async_computation.23 | async-start | bytes 5242880 | tf_op jit(solution)/shard_map/reduce_scatter | solution.py:33
  376.6 243.6 %all-gather.31.cloned.1.call-start = ((), (), s32[]{:S(2)}) async-start(), calls=%async_computation.20 | async-start | bytes 5242880 | tf_op jit(solution)/shard_map/all_gather | solution.py:29
  506.7 267.0 %all-gather.57.cloned.1.call-start = ((), (), s32[]{:S(2)}) async-start(), calls=%async_computation.48 | async-start | bytes 5242880 | tf_op jit(solution)/shard_map/all_gather | solution.py:39
  509.9 344.6 %all-gather.35.cloned.1.call-start = ((), (), s32[]{:S(2)}) async-start(), calls=%async_computation.24 | async-start | bytes 5242880 | tf_op jit(solution)/shard_map/all_gather | solution.py:29
  510.5 424.7 %all-gather.59.cloned.1.call-start = ((), (), s32[]{:S(2)}) async-start(), calls=%async_computation.49 | async-start | bytes 5242880 | tf_op jit(solution)/shard_map/all_gather | solution.py:39
  511.1 501.6 %reduce-scatter.31.cloned.1.call-start = ((), (), s32[]{:S(2)}) async-start(), calls=%async_computation.26 | async-start | bytes 5242880 | tf_op jit(solution)/shard_map/reduce_scatter | solution.py:43
  797.3 295.0 %reduce-scatter.35.cloned.1.call-start = ((), (), s32[]{:S(2)}) async-start(), calls=%async_computation.29 | async-start | bytes 5242880 | tf_op jit(solution)/shard_map/reduce_scatter | solution.py:43
  967.9 290.6 %all-gather.37.cloned.1.call-start = ((), (), s32[]{:S(2)}) async-start(), calls=%async_computation.27 | async-start | bytes 5242880 | tf_op jit(solution)/shard_map/all_gather | solution.py:39
  1177.8 333.2 %reduce-scatter.53.cloned.1.call-start = ((), (), s32[]{:S(2)}) async-start(), calls=%async_computation.39 | async-start | bytes 3981312 | tf_op jit(solution)/shard_map/reduce_scatter | solution.py:277
  1189.5 323.5 %reduce-scatter.51.cloned.1.call-start = ((), (), s32[]{:S(2)}) async-start(), calls=%async_computation.38 | async-start | bytes 3981312 | tf_op jit(solution)/shard_map/reduce_scatter | solution.py:274
  1201.8 313.3 %reduce-scatter.49.cloned.1.call-start = ((), (), s32[]{:S(2)}) async-start(), calls=%async_computation.37 | async-start | bytes 3981312 | tf_op jit(solution)/shard_map/reduce_scatter | solution.py:271
  1213.6 318.5 %reduce-scatter.57.cloned.1.call-start = ((), (), s32[]{:S(2)}) async-start(), calls=%async_computation.51 | async-start | bytes 589824
  1214.8 361.6 %reduce-scatter.41.cloned.1.call-start = ((), (), s32[]{:S(2)}) async-start(), calls=%async_computation.33 | async-start | bytes 2359296 | tf_op jit(solution)/shard_map/reduce_scatter | solution.py:259
  1372.0 249.7 %reduce-scatter.39.cloned.1.call-start = ((), (), s32[]{:S(2)}) async-start(), calls=%async_computation.32 | async-start | bytes 2359296 | tf_op jit(solution)/shard_map/reduce_scatter | solution.py:256
  1385.3 288.0 %reduce-scatter.47.cloned.1.call-start = ((), (), s32[]{:S(2)}) async-start(), calls=%async_computation.36 | async-start | bytes 3981312 | tf_op jit(solution)/shard_map/reduce_scatter | solution.py:268
  1396.6 328.3 %reduce-scatter.43.cloned.1.call-start = ((), (), s32[]{:S(2)}) async-start(), calls=%async_computation.34 | async-start | bytes 3981312 | tf_op jit(solution)/shard_map/reduce_scatter | solution.py:262
  1415.4 360.9 %reduce-scatter.45.cloned.1.call-start = ((), (), s32[]{:S(2)}) async-start(), calls=%async_computation.35 | async-start | bytes 3981312 | tf_op jit(solution)/shard_map/reduce_scatter | solution.py:265
  1428.3 427.7 %reduce-scatter.33.cloned.1.call-start = ((), (), s32[]{:S(2)}) async-start(), calls=%async_computation.28 | async-start | bytes 5242880 | tf_op jit(solution)/shard_map/reduce_scatter | solution.py:43
  1465.2 470.4 %reduce-scatter.37.cloned.1.call-start = ((), (), s32[]{:S(2)}) async-start(), calls=%async_computation.31 | async-start | bytes 5242880 | tf_op jit(solution)/shard_map/reduce_scatter | solution.py:43
  1501.1 514.0 %reduce-scatter.25.cloned.1.call-start = ((), (), s32[]{:S(2)}) async-start(), calls=%async_computation.21 | async-start | bytes 5242880 | tf_op jit(solution)/shard_map/reduce_scatter | solution.py:33
  1510.8 542.4 %reduce-scatter.55.cloned.1.call-start = ((), (), s32[]{:S(2)}) async-start(), calls=%async_computation.50 | async-start | bytes 589824
  (128 other events, 7822.8 us)
Sparse Core Ops, SparseCore 0:
  42.7 80.7 all-gather.28
  262.3 80.7 all-gather.32
  345.4 75.2 reduce-scatter.22
  423.1 77.2 reduce-scatter.26
  539.4 80.7 all-gather.30
  692.9 80.7 all-gather.56
  775.1 79.2 all-gather.34
  855.9 79.2 all-gather.58
  937.4 75.2 reduce-scatter.30
  1014.9 77.2 reduce-scatter.34
  1094.5 77.2 reduce-scatter.28
  1177.2 81.2 all-gather.36
  1260.1 79.2 all-gather.38
  1343.3 46.6 reduce-scatter.52
  1393.9 48.0 reduce-scatter.50
  1445.8 48.0 reduce-scatter.48
  1535.2 41.1 reduce-scatter.40
  1580.4 41.2 reduce-scatter.38
  1625.2 48.0 reduce-scatter.46
  1676.8 48.0 reduce-scatter.42
  1728.2 48.0 reduce-scatter.44
  1779.2 76.7 reduce-scatter.32
  1858.4 77.2 reduce-scatter.36
  1937.8 77.2 reduce-scatter.24
  (10 shorter events, 331.5 us)
where the time goes:
time: 2090 us; the launch traced here: 2080 us
  waiting for transfers between devices  1580 us (76%)
  matrix products  352 us (17%)
  other arithmetic  65.8 us (3%)
  blocking collectives  38.6 us (2%)
  local copies, waits for them, and re-layouts  28.2 us (1%)
    all_gather x4, waiting for transfers between devices, spread_rows(): return lax.all_gather(normed_rows, 'tensor', axis=1, tiled=True)  296 us
    reduce_scatter x4, waiting for transfers between devices, collect_grads(): lax.psum_scatter(partial_value.astype(jnp.bfloat16), 'tensor', scatter_di...  282 us
    reduce_scatter x4, waiting for transfers between devices, collect_rows(): lax.psum_scatter(partial_value.astype(jnp.bfloat16), 'tensor', scatter_di...  261 us
    all_gather x4, waiting for transfers between devices, spread_grads(): return lax.all_gather(grad_rows, 'tensor', axis=1, tiled=True)  261 us
    dot_general x16, matrix products, project(): jnp.einsum('bsd,de->bse', in_rows, weight_mat, preferred_element_type=jnp...  107 us
    dot_general x12, matrix products, project_back(): jnp.einsum('bse,de->bsd', grad_rows, weight_mat, preferred_element_type=j...  92.7 us
    dot_general x16, matrix products, weight_grad(): jnp.einsum('bsd,bse->de', in_rows, grad_rows, preferred_element_type=jnp....  78.7 us
    unnamed x36, waiting for transfers between devices  52.5 us
  transfers between devices with their start and end apart: 34, of which 31 were waited for; matrix products, arithmetic and copies ran while one was open for 20% of the time, Pallas kernels for 0%

commit v1 on v0

--- a/solution.py
+++ b/solution.py
@@ -1,6 +1,9 @@
+import functools
 import jax
 import jax.numpy as jnp
 from jax import lax
+from jax.experimental import pallas as pl
+from jax.experimental.pallas import tpu as pltpu
 from jax.sharding import PartitionSpec as P
 
 DK = 256
@@ -303,33 +306,1076 @@
     )
 
 
+def cost(flops, bytes_accessed, transcendentals):
+    return pl.CostEstimate(int(flops*0.3)+1, 0, int(bytes_accessed*0.3)+1)
+
+
+F32, BF16 = jnp.float32, jnp.bfloat16
+
+
+def dot_nt(a, b):
+    return lax.dot_general(a, b, (((1,), (1,)), ((), ())), preferred_element_type=F32)
+
+
+def dot_nn(a, b):
+    return lax.dot_general(a, b, (((1,), (0,)), ((), ())), preferred_element_type=F32)
+
+
+def dot_tn(a, b):
+    return lax.dot_general(a, b, (((0,), (0,)), ((), ())), preferred_element_type=F32)
+
+
+PARAMS = pltpu.CompilerParams(vmem_limit_bytes=48 * 1024 * 1024)
+GELU_A = 0.7978845608028654
+GELU_B = 0.044715
+VM = pl.BlockSpec(memory_space=pltpu.VMEM)
+SM = pl.BlockSpec(memory_space=pltpu.SMEM)
+ANY = pl.BlockSpec(memory_space=pl.ANY)
+
+
+def by_case(value, count, body):
+    for case in range(count):
+
+        @pl.when(value == case)
+        def _(case=case):
+            body(case)
+
+
+def shape_of(shape, dtype):
+    return jax.ShapeDtypeStruct(shape, dtype)
+
+
+def weight_copies(pieces, first, last, held, sems):
+    width = pieces[0].shape[1]
+    return [
+        pltpu.make_async_copy(
+            piece.at[pl.ds(first, last - first)], held.at[:, pl.ds(p * width, width)], sems.at[p]
+        )
+        for p, piece in enumerate(pieces)
+    ]
+
+
+def ffn_kernel(dv, first, x_ref, c_ref, f0, f1, f2, f3, act_ref, held, sems):
+    copies = weight_copies((f0, f1, f2, f3), 0, 3 * dv, held, sems)
+    for copy in copies:
+        copy.start()
+    for copy in copies:
+        copy.wait()
+    act = dot_nt(held[:dv], x_ref[...])
+    lin = dot_nt(held[dv : 2 * dv], x_ref[...])
+    grad_hidden = dot_nt(held[2 * dv :], c_ref[first : first + x_ref.shape[0]])
+    square = act * act
+    tanh = jnp.tanh(GELU_A * (act + GELU_B * (square * act)))
+    gelu = 0.5 * act * (1.0 + tanh)
+    slope = 0.5 * (1.0 + tanh) + 0.5 * act * (1.0 - tanh * tanh) * (
+        GELU_A * (1.0 + 3.0 * GELU_B * square)
+    )
+    act_ref[:dv] = (grad_hidden * lin * slope).astype(BF16)
+    act_ref[dv : 2 * dv] = (grad_hidden * gelu).astype(BF16)
+    act_ref[2 * dv :] = (gelu * lin).astype(BF16)
+
+
+def ffn_block(x, cot, pieces, half):
+    tokens, dv, width = x.shape[0], pieces[0].shape[0] // 3, pieces[0].shape[1]
+    return pl.pallas_call(
+        functools.partial(ffn_kernel, dv, half * tokens),
+        out_shape=shape_of((3 * dv, tokens), BF16),
+        in_specs=[VM, VM] + [ANY] * 4,
+        out_specs=VM,
+        scratch_shapes=[pltpu.VMEM((3 * dv, 4 * width), BF16), pltpu.SemaphoreType.DMA((4,))],
+        compiler_params=PARAMS,
+        cost_estimate=cost(
+            flops=24 * tokens * dv * width, bytes_accessed=12 << 20, transcendentals=tokens * dv
+        ),
+        name="ffn_block",
+    )(x, cot, *pieces)
+
+
+def ffn_grad_kernel(dv, x0, x1, c_ref, a0, a1, *outs):
+    side = outs[0].shape[1]
+    half = x0.shape[0]
+    for p, target in enumerate(outs):
+        cols = slice(p * side, (p + 1) * side)
+        for k in range(3):
+            rows = slice(k * dv, (k + 1) * dv)
+            parts = (c_ref[:half, cols], c_ref[half:, cols]) if k == 2 else (x0[:, cols], x1[:, cols])
+            target[rows] = (dot_nn(a0[rows], parts[0]) + dot_nn(a1[rows], parts[1])).astype(BF16)
+
+
+def ffn_grad_block(xs, cot, acts):
+    rows, side = acts[0].shape[0], cot.shape[1] // 4
+    grads = shape_of((rows, side), BF16)
+    return pl.pallas_call(
+        functools.partial(ffn_grad_kernel, rows // 3),
+        out_shape=(grads,) * 4,
+        in_specs=[VM] * 5,
+        out_specs=(VM,) * 4,
+        compiler_params=PARAMS,
+        cost_estimate=cost(
+            flops=8 * cot.shape[0] * rows * side, bytes_accessed=16 << 20, transcendentals=0
+        ),
+        name="ffn_grad_block",
+    )(*xs, cot, *acts)
+
+
+def decays(rate, keys, queries):
+    down = jnp.exp(-keys.astype(F32) * rate) * 0.0625
+    up = jnp.exp(queries.astype(F32) * rate)
+    return jnp.where(queries >= keys, down * up, 0.0)
+
+
+def log_rate(spots_ref):
+    return jnp.log(1.0 - jnp.exp2(jnp.full((1, 1), -5.0, F32) - spots_ref[0].astype(F32)))
+
+
+def tiles_of(x, length):
+    half = length // 2
+    early = slice(x * half, (x + 1) * half)
+    late = slice((1 - x) * half, (2 - x) * half)
+    lanes = lax.broadcasted_iota(jnp.int32, (1, half), 1)
+    below = lax.broadcasted_iota(jnp.int32, (half, 1), 0)
+    every = lax.broadcasted_iota(jnp.int32, (length, 1), 0)
+    every = lax.rem(every + x * half, length)
+    return (
+        (early, early, below, lanes),
+        (slice(None), late, every, lanes + half),
+    )
+
+
+def mix_kernel(
+    dk, dv, spots_ref, x_ref, m0, m1, m2, m3, vqk_ref, g_ref, nrm_ref, inv_ref, out_ref, held, sems
+):
+    copies = weight_copies((m0, m1, m2, m3), dv, 3 * dv + 2 * dk, held, sems)
+    for copy in copies:
+        copy.start()
+    for copy in copies:
+        copy.wait()
+    length = x_ref.shape[0]
+    tile = 512
+
+    def step(i, carry):
+        rows = pl.ds(pl.multiple_of(i * tile, tile), tile)
+        g_ref[:, rows] = dot_nt(held[:dv], x_ref[rows])
+        vqk_ref[:, rows] = dot_nt(held[dv:], x_ref[rows]).astype(BF16)
+        return carry
+
+    lax.fori_loop(0, length // tile, step, 0)
+    rate = log_rate(spots_ref)
+
+    def attend(x):
+        for keys, queries, key_spots, query_spots in tiles_of(x, length):
+            scores = dot_tn(vqk_ref[dv + dk :, keys], vqk_ref[dv : dv + dk, queries])
+            weights = (scores * decays(rate, key_spots, query_spots)).astype(BF16)
+            retained = dot_nn(vqk_ref[:dv, keys], weights)
+            inv = lax.rsqrt(jnp.mean(retained * retained, axis=0, keepdims=True) + 1.0)
+            nrm = retained * inv
+            gate = g_ref[:, queries]
+            nrm_ref[:, queries] = nrm
+            inv_ref[:, queries] = inv
+            out_ref[:, queries] = (gate / (1.0 + jnp.exp(-gate)) * nrm).astype(BF16)
+
+    by_case(spots_ref[1], 2, attend)
+
+
+def mix_block(spots, x, pieces, dk, dv):
+    tokens, width = x.shape[0], pieces[0].shape[1]
+    return pl.pallas_call(
+        functools.partial(mix_kernel, dk, dv),
+        out_shape=(
+            shape_of((dv + 2 * dk, tokens), BF16),
+            shape_of((dv, tokens), F32),
+            shape_of((dv, tokens), F32),
+            shape_of((1, tokens), F32),
+            shape_of((dv, tokens), BF16),
+        ),
+        in_specs=[SM, VM] + [ANY] * 4,
+        out_specs=(VM,) * 5,
+        scratch_shapes=[
+            pltpu.VMEM((2 * dv + 2 * dk, 4 * width), BF16),
+            pltpu.SemaphoreType.DMA((4,)),
+        ],
+        compiler_params=PARAMS,
+        cost_estimate=cost(
+            flops=2 * tokens * (2 * dk + 2 * dv) * x.shape[1] + 2 * tokens * tokens * (dk + dv),
+            bytes_accessed=17 << 20,
+            transcendentals=tokens * dv,
+        ),
+        name="mix_block",
+    )(spots, x, *pieces)
+
+
+def mix_back_kernel(
+    dk, dv, spots_ref, s0, s1, m0, m1, m2, m3, vqk_ref, g_ref, nrm_ref, inv_ref,
+    grad_ref, held, dv_ref, dk_ref, rg_ref, sems
+):
+    copies = weight_copies((m0, m1, m2, m3), 0, dv, held, sems)
+    for copy in copies:
+        copy.start()
+    for copy in copies:
+        copy.wait()
+    half = s0.shape[0]
+    length = 2 * half
+    q_rows, k_rows = slice(2 * dv, 2 * dv + dk), slice(2 * dv + dk, 2 * dv + 2 * dk)
+    for i, s_ref in enumerate((s0, s1)):
+        rows = slice(i * half, (i + 1) * half)
+        merged_grad = dot_nt(held[...], s_ref[...])
+        gate, nrm = g_ref[:, rows], nrm_ref[:, rows]
+        sig = 1.0 / (1.0 + jnp.exp(-gate))
+        grad_ref[:dv, rows] = (merged_grad * nrm * (sig * (1.0 + gate * (1.0 - sig)))).astype(BF16)
+        normed_grad = merged_grad * (gate * sig)
+        mean = jnp.mean(normed_grad * nrm, axis=0, keepdims=True)
+        rg_ref[:, rows] = (inv_ref[:, rows] * (normed_grad - nrm * mean)).astype(BF16)
+    rate = log_rate(spots_ref)
+    def attend(x):
+        early, late = tiles_of(x, length)
+        for keys, queries, key_spots, query_spots in (late, early):
+            decay = decays(rate, key_spots, query_spots)
+            k_part, q_part = vqk_ref[dv + dk :, keys], vqk_ref[dv : dv + dk, queries]
+            rg_part = rg_ref[:, queries]
+            weights = (dot_tn(k_part, q_part) * decay).astype(BF16)
+            score_grad = (dot_tn(vqk_ref[:dv, keys], rg_part) * decay).astype(BF16)
+            grad_ref[q_rows, queries] = dot_nn(k_part, score_grad).astype(BF16)
+            values_grad = dot_nt(rg_part, weights)
+            keys_grad = dot_nt(q_part, score_grad)
+            if keys == slice(None):
+                dv_ref[...] = values_grad
+                dk_ref[...] = keys_grad
+            else:
+                dv_ref[:, keys] += values_grad
+                dk_ref[:, keys] += keys_grad
+
+    by_case(spots_ref[1], 2, attend)
+    grad_ref[dv : 2 * dv] = dv_ref[...].astype(BF16)
+    grad_ref[k_rows] = dk_ref[...].astype(BF16)
+
+
+def mix_back_block(spots, sides, pieces, kept, dk, dv):
+    tokens, width = 2 * sides[0].shape[0], pieces[0].shape[1]
+    return pl.pallas_call(
+        functools.partial(mix_back_kernel, dk, dv),
+        out_shape=shape_of((2 * dv + 2 * dk, tokens), BF16),
+        in_specs=[SM, VM, VM] + [ANY] * 4 + [VM] * 4,
+        out_specs=VM,
+        scratch_shapes=[
+            pltpu.VMEM((dv, 4 * width), BF16),
+            pltpu.VMEM((dv, tokens), F32),
+            pltpu.VMEM((dk, tokens), F32),
+            pltpu.VMEM((dv, tokens), BF16),
+            pltpu.SemaphoreType.DMA((4,)),
+        ],
+        compiler_params=PARAMS,
+        cost_estimate=cost(
+            flops=8 * tokens * dv * width + 2 * tokens * tokens * (2 * dv + 3 * dk),
+            bytes_accessed=16 << 20,
+            transcendentals=tokens * dv,
+        ),
+        name="mix_back_block",
+    )(spots, *sides, *pieces, *kept)
+
+
+def mix_grad_kernel(dv, s0, s1, x_ref, out_ref, grad_ref, *outs):
+    side = outs[0].shape[1]
+    count, half = grad_ref.shape[0], s0.shape[0]
+    for p, target in enumerate(outs):
+        cols = slice(p * side, (p + 1) * side)
+        target[:dv] = (
+            dot_nn(out_ref[:, :half], s0[:, cols]) + dot_nn(out_ref[:, half:], s1[:, cols])
+        ).astype(BF16)
+        for rows in (slice(0, dv), slice(dv, 2 * dv), slice(2 * dv, count)):
+            target[dv + rows.start : dv + rows.stop] = dot_nn(
+                grad_ref[rows], x_ref[:, cols]
+            ).astype(BF16)
+
+
+def mix_grad_block(sides, x, merged, grads):
+    dv, side = merged.shape[0], x.shape[1] // 4
+    rows = dv + grads.shape[0]
+    out = shape_of((rows, side), BF16)
+    return pl.pallas_call(
+        functools.partial(mix_grad_kernel, dv),
+        out_shape=(out,) * 4,
+        in_specs=[VM] * 5,
+        out_specs=(VM,) * 4,
+        compiler_params=PARAMS,
+        cost_estimate=cost(
+            flops=8 * x.shape[0] * rows * side, bytes_accessed=20 << 20, transcendentals=0
+        ),
+        name="mix_grad_block",
+    )(*sides, x, merged, grads)
+
+
+def sum_kernel(n_blocks, source_first, first, count, lanes, *refs):
+    sources, pieces = refs[:n_blocks], refs[n_blocks : 5 * n_blocks]
+    out_ref, held_source, held, source_sems, sems = refs[5 * n_blocks :]
+    width = held.shape[2]
+
+    def into(j):
+        return pl.ds(j * count, count)
+
+    early = [
+        pltpu.make_async_copy(
+            sources[j].at[pl.ds(source_first, count), lanes], held_source.at[into(j)], source_sems.at[j]
+        )
+        for j in range(n_blocks)
+    ]
+    copies = [
+        [
+            pltpu.make_async_copy(
+                pieces[4 * j + p].at[pl.ds(first, count)], held.at[p, into(j)], sems.at[p, j]
+            )
+            for j in range(n_blocks)
+        ]
+        for p in range(4)
+    ]
+    for copy in early + [copy for group in copies for copy in group]:
+        copy.start()
+    for copy in early:
+        copy.wait()
+    for p in range(4):
+        for copy in copies[p]:
+            copy.wait()
+        out_ref[:, p * width : (p + 1) * width] = dot_tn(held_source[...], held[p]).astype(
+            out_ref.dtype
+        )
+
+
+def sum_blocks(sources, blocks, source_first, first, count, half, out_type):
+    tokens, width, n = sources[0].shape[1], blocks[0][0].shape[1], len(blocks)
+    if half is None:
+        half = 0
+    else:
+        tokens = tokens // 2
+    return pl.pallas_call(
+        functools.partial(
+            sum_kernel, n, source_first, first, count, pl.ds(half * tokens, tokens)
+        ),
+        out_shape=shape_of((tokens, 4 * width), out_type),
+        in_specs=[ANY] * (5 * n),
+        out_specs=VM,
+        scratch_shapes=[
+            pltpu.VMEM((n * count, tokens), BF16),
+            pltpu.VMEM((4, n * count, width), BF16),
+            pltpu.SemaphoreType.DMA((n,)),
+            pltpu.SemaphoreType.DMA((4, n)),
+        ],
+        compiler_params=PARAMS,
+        cost_estimate=cost(
+            flops=8 * tokens * count * n * width,
+            bytes_accessed=8 * count * n * width + 2 * count * n * tokens + 16 * tokens * width,
+            transcendentals=0,
+        ),
+        name="sum_blocks",
+    )(*sources, *[piece for block in blocks for piece in block])
+
+
+def piece_of(p, y, c):
+    return 4 * ((p // 2 % 2) ^ y) + 2 * (p % 2) + ((p // 4) ^ c)
+
+
+def spots_of(x, y, c, z):
+    return jnp.stack([x, y, c, z]).astype(jnp.int32)
+
+
+def split_kernel(at, local, *outs):
+    z = at[3]
+    width = local.shape[2] // 8
+
+    def split(case):
+        for k, out in enumerate(outs):
+            micro = lax.rem(z - k + 4, 4) // 2
+            for p in range(8):
+                first = piece_of(p, case // 2, case % 2) * width
+                out[:, p * width : (p + 1) * width] = local[micro, :, first : first + width]
+
+    by_case(2 * at[1] + at[2], 4, split)
+
+
+def split_blocks(at, local):
+    block = shape_of(local.shape[1:], local.dtype)
+    return pl.pallas_call(
+        split_kernel,
+        out_shape=(block,) * 4,
+        in_specs=[SM, VM],
+        out_specs=(VM,) * 4,
+        compiler_params=PARAMS,
+        cost_estimate=cost(flops=1196000000, bytes_accessed=3 * local.size * 2, transcendentals=0),
+        name="split_blocks",
+    )(at, local)
+
+
+EPS = 1e-6
+
+
+def assemble_kernel(normed, at, *refs):
+    blocks, others = refs[:4], refs[4:8]
+    x, c, z = at[0], at[2], at[3]
+    here = ((z ^ c) & 1) == x
+    count = blocks[0].shape[0]
+
+    def put(sources):
+        for k, source in enumerate(sources):
+            spot = lax.rem(z + k - 2 * x + 4, 4)
+            rows = pl.ds(pl.multiple_of(spot * count, count), count)
+            if normed:
+                gains, own, out = refs[8:]
+                values = source[...].astype(F32)
+                scale = lax.rsqrt(jnp.mean(values * values, axis=-1, keepdims=True) + EPS)
+                out[rows] = (values * scale * gains[0:1]).astype(BF16)
+
+                @pl.when(spot < 2)
+                def _():
+                    own[pl.ds(pl.multiple_of(lax.rem(spot, 2) * count, count), count)] = source[...]
+
+            else:
+                refs[8][rows] = source[...]
+
+    @pl.when(here)
+    def _():
+        put(blocks)
+
+    @pl.when(jnp.logical_not(here))
+    def _():
+        put(others)
+
+
+def assemble(at, blocks, others, gains=None):
+    count, width = blocks[0].shape
+    whole, half = shape_of((4 * count, width), BF16), shape_of((2 * count, width), BF16)
+    extra = [] if gains is None else [gains]
+    return pl.pallas_call(
+        functools.partial(assemble_kernel, gains is not None),
+        out_shape=whole if gains is None else (half, whole),
+        in_specs=[SM] + [VM] * (8 + len(extra)),
+        out_specs=VM if gains is None else (VM, VM),
+        compiler_params=PARAMS,
+        cost_estimate=cost(
+            flops=3380000000, bytes_accessed=24 * count * width, transcendentals=0
+        ),
+        name="assemble",
+    )(at, *blocks, *others, *extra)
+
+
+def middle_kernel(stream, partial, got, gains, middle, normed):
+    tile = 128
+
+    def step(i, carry):
+        rows = pl.ds(pl.multiple_of(i * tile, tile), tile)
+        values = stream[rows].astype(F32) + partial[rows] + got[rows].astype(F32)
+        middle[rows] = values
+        scale = lax.rsqrt(jnp.mean(values * values, axis=-1, keepdims=True) + EPS)
+        normed[rows] = (values * scale * gains[1:2]).astype(BF16)
+        return carry
+
+    lax.fori_loop(0, stream.shape[0] // tile, step, 0)
+
+
+def middle_block(stream, partial, got, gains):
+    return pl.pallas_call(
+        middle_kernel,
+        out_shape=(shape_of(stream.shape, F32), shape_of(stream.shape, BF16)),
+        in_specs=[VM] * 4,
+        out_specs=(VM, VM),
+        compiler_params=PARAMS,
+        cost_estimate=cost(flops=3796000000, bytes_accessed=14 * stream.size, transcendentals=0),
+        name="middle_block",
+    )(stream, partial, got, gains)
+
+
+def norm_back_kernel(row, base, partial, got, grad, gains, *outs):
+    tile = 128
+    total_ref = outs[0]
+    total_ref[...] = jnp.zeros_like(total_ref)
+    gain = gains[row : row + 1]
+
+    def step(i, carry):
+        rows = pl.ds(pl.multiple_of(i * tile, tile), tile)
+        values = base[rows].astype(F32)
+        grad_norm = partial[rows] + got[rows].astype(F32)
+        scale = lax.rsqrt(jnp.mean(values * values, axis=-1, keepdims=True) + EPS)
+        unit = values * scale
+        total_ref[...] += jnp.sum(grad_norm * unit, axis=0, keepdims=True)
+        inner = grad_norm * gain
+        mean = jnp.mean(inner * unit, axis=-1, keepdims=True)
+        result = grad[rows].astype(F32) + scale * (inner - unit * mean)
+        for out in outs[1:]:
+            out[rows] = result.astype(out.dtype)
+        return carry
+
+    lax.fori_loop(0, base.shape[0] // tile, step, 0)
+
+
+def norm_back_block(row, base, partial, got, grad, gains, types):
+    return pl.pallas_call(
+        functools.partial(norm_back_kernel, row),
+        out_shape=(shape_of((1, base.shape[1]), F32),)
+        + tuple(shape_of(base.shape, kind) for kind in types),
+        in_specs=[VM] * 5,
+        out_specs=(VM,) * (1 + len(types)),
+        compiler_params=PARAMS,
+        cost_estimate=cost(flops=5200000000, bytes_accessed=20 * base.size, transcendentals=0),
+        name="norm_back_block",
+    )(base, partial, got, grad, gains)
+
+
+def spread_kernel(at, own, *refs):
+    x, z = at[0], at[3]
+    count = refs[0].shape[0]
+    for k, out in enumerate(refs[2:]):
+        block = lax.rem(z + k, 4)
+        rows = pl.ds(pl.multiple_of(lax.rem(block, 2) * count, count), count)
+
+        @pl.when(block // 2 == x)
+        def _(out=out, rows=rows):
+            out[...] = own[rows]
+
+        for part in range(2):
+
+            @pl.when((block // 2 != x) & (lax.rem(block, 2) == part))
+            def _(out=out, other=refs[part]):
+                out[...] = other[...]
+
+
+def spread_blocks(at, own, others):
+    block = shape_of((own.shape[0] // 2, own.shape[1]), own.dtype)
+    return pl.pallas_call(
+        spread_kernel,
+        out_shape=(block,) * 4,
+        in_specs=[SM, VM, VM, VM],
+        out_specs=(VM,) * 4,
+        compiler_params=PARAMS,
+        cost_estimate=cost(flops=1820000000, bytes_accessed=8 * own.size, transcendentals=0),
+        name="spread_blocks",
+    )(at, own, *others)
+
+
+def finish_kernel(at, b0, b1, b2, b3, out):
+    x, y, c, z = (at[i] for i in range(4))
+    width = out.shape[2] // 8
+    for micro in range(2):
+        source = lax.rem(z - 2 * micro - (x ^ c) + 8, 4)
+        for k, block in enumerate((b0, b1, b2, b3)):
+
+            @pl.when(source == k)
+            def _(block=block, micro=micro):
+                def put(case):
+                    for p in range(8):
+                        first = piece_of(p, case // 2, case % 2) * width
+                        out[micro, :, first : first + width] = block[
+                            :, p * width : (p + 1) * width
+                        ].astype(out.dtype)
+
+                by_case(2 * y + c, 4, put)
+
+
+def finish_tokens(at, blocks, kind):
+    count, width = blocks[0].shape
+    return pl.pallas_call(
+        finish_kernel,
+        out_shape=shape_of((2, count, width), kind),
+        in_specs=[SM] + [VM] * 4,
+        out_specs=VM,
+        compiler_params=PARAMS,
+        cost_estimate=cost(flops=1560000000, bytes_accessed=16 * count * width, transcendentals=0),
+        name="finish_tokens",
+    )(at, *blocks)
+
+
+def rows_kernel(spans, turned, at, mine, got, *refs):
+    outs, held = refs[: len(spans)], refs[len(spans)]
+
+    def put(x):
+        for out, (first, count), turn in zip(outs, spans, turned):
+            target = held if turn else out
+            rows = slice(first, first + count)
+            target[x * count : (x + 1) * count] = mine[rows].astype(F32)
+            target[(1 - x) * count : (2 - x) * count] = got[rows].astype(F32)
+            if turn:
+                out[...] = held[...].T
+
+    by_case(at[0], 2, put)
+
+
+def finish_rows(at, mine, got, spans, turned):
+    width = mine.shape[1]
+    shapes = [(2 * n, width) for _, n in spans]
+    held = max([n for (_, n), turn in zip(spans, turned) if turn] + [8])
+    return pl.pallas_call(
+        functools.partial(rows_kernel, spans, turned),
+        out_shape=tuple(
+            shape_of(s[::-1] if turn else s, F32) for s, turn in zip(shapes, turned)
+        ),
+        in_specs=[SM, VM, VM],
+        out_specs=(VM,) * len(spans),
+        scratch_shapes=[pltpu.VMEM((2 * held, width), F32)],
+        compiler_params=PARAMS,
+        cost_estimate=cost(flops=1560000000, bytes_accessed=12 * mine.size, transcendentals=0),
+        name="finish_rows",
+    )(at, mine, got)
+
+
+O = {'xd': 2, 'yd': 1, 'zd': 2, 'scale': 0.3, 'back': ['B1', 'h3', 'r1', 'u2', 'B2', '|', 'r0', 'x1', 'v1', 'H0', 'x3', 'x2', 'u3', 'B3', 'A', '|', '|', 'Q0', 'v2', 'H1', 'D', '|', 'v3', 'H2', 'L', 'U0', 'U1', 'W', 'e0', 'e1', 'H3', 'f1', 'f0', 'U2', '|', 'f2', 'U3', 'f3', 's', '|', 'Q1', 'e2', 'g1', 't1', 'e3', 'g2', 'm', '|', 't2', 'c1', 'p1', 'c2', 'p2', 'n', 'g3', 't3', 'g0', 't0', 'o', 'c3', '|', '|', 'Q2', 'w', 'p3', 'a1', 'b1', 'T1', 'X', 'c0', 'a2', 'p0', 'b2', 'T2', '|', 'C1', 'Z2', 'a3', 'a0', 'b3', 'T3', '|', 'C2', 'P1', 'P2', 'i', 'b0', 'T0', '|', 'C3', 'P3', 'Q3', 'j', 'k', 'C0', '|', '|', 'G2', 'E0', 'P0', 'M', 'F', 'E1']}
+
+
+SWAP = ((0, 1), (1, 0))
+RING = ((0, 1), (1, 2), (2, 3), (3, 0))
+XCZ = ("x", "c", "z")
+ORDER = (1, 2, 3, 0)
+
+
+def prepare_kernel(dk, dv, x_ref, q, k, v, g, o, a, n, d, gains, m_own, m_send, f_own, f_send, turned):
+    def put(x, source, own, send, first, count):
+        own[first : first + count] = source[x * count : (x + 1) * count]
+        send[first : first + count] = source[(1 - x) * count : (2 - x) * count]
+
+    def put_all(x):
+        put(x, o, m_own, m_send, 0, dv)
+        put(x, g, m_own, m_send, dv, dv)
+        put(x, v, m_own, m_send, 2 * dv, dv)
+        for i, source in enumerate((q, k)):
+            turned[...] = source[...].T
+            put(x, turned, m_own, m_send, 3 * dv + i * dk, dk)
+        put(x, a, f_own, f_send, 0, dv)
+        put(x, n, f_own, f_send, dv, dv)
+        put(x, d, f_own, f_send, 2 * dv, dv)
+
+    by_case(x_ref[0], 2, put_all)
+    m_own[3 * dv + 2 * dk :] = gains[...]
+    m_send[3 * dv + 2 * dk :] = gains[...]
+
+
+def prepare(at, weights, gains, dk, dv):
+    width = gains.shape[1]
+    mix = shape_of((3 * dv + 2 * dk + 16, width), BF16)
+    ffn = shape_of((3 * dv, width), BF16)
+    return pl.pallas_call(
+        functools.partial(prepare_kernel, dk, dv),
+        out_shape=(mix, mix, ffn, ffn),
+        in_specs=[SM] + [VM] * 9,
+        out_specs=(VM,) * 4,
+        scratch_shapes=[pltpu.VMEM((2 * dk, width), BF16)],
+        compiler_params=PARAMS,
+        name="prepare",
+    )(at, *weights, gains)
+
+
+def join_kernel(at, own, got, out):
+    width = own.shape[1]
+
+    def put(x):
+        out[:, x * width : (x + 1) * width] = own[...]
+        out[:, (1 - x) * width : (2 - x) * width] = got[...]
+
+    by_case(at[0], 2, put)
+
+
+def join(at, own, got):
+    return pl.pallas_call(
+        join_kernel,
+        out_shape=shape_of((own.shape[0], 2 * own.shape[1]), BF16),
+        in_specs=[SM, VM, VM],
+        out_specs=VM,
+        compiler_params=PARAMS,
+        name="join",
+    )(at, own, got)
+
+
+def tie(value, *others):
+    return lax.optimization_barrier((value,) + others)[0]
+
+
+class Fence:
+    def __init__(self):
+        self.before, self.now = (), []
+
+    def close(self, *more):
+        self.before, self.now = tuple(self.now) + more, []
+
+
+class Link:
+    def __init__(self, fence, depth=1):
+        self.fence, self.depth, self.ended = fence, depth, []
+
+    def group(self, sends, *after, fenced=True):
+        wait = self.ended[-self.depth] if len(self.ended) >= self.depth else ()
+        if fenced:
+            wait = wait + self.fence.before
+        results = []
+        for array, axis, pairs in sends:
+            if wait + after:
+                array = tie(array, *wait, *after)
+            results.append(lax.ppermute(array, axis, pairs))
+        self.ended.append(tuple(results))
+        if fenced:
+            self.fence.now += results
+        return results
+
+    def send(self, array, axis, pairs, *after):
+        return self.group([(array, axis, pairs)], *after)[0]
+
+    def swap(self, array, axis, *after):
+        return self.send(array, axis, SWAP, *after)
+
+
+def add(*terms):
+    total = terms[0].astype(F32)
+    for term in terms[1:]:
+        total = total + term.astype(F32)
+    return total.astype(BF16)
+
+
+def pick(pair, index):
+    return jnp.where(index == 0, pair[0], pair[1])
+
+
+def home_pairs():
+    pairs = []
+    for c in range(2):
+        for z in range(4):
+            home = (z ^ c) & 1
+            pairs.append((home * 8 + c * 4 + z, (1 - home) * 8 + c * 4 + z))
+    return pairs
+
+
+def round_pairs(shift):
+    pairs = []
+    for x in range(2):
+        for c in range(2):
+            for z in range(4):
+                if (z & 1) == (x ^ c):
+                    pairs.append((x * 8 + c * 4 + (z + shift) % 4, x * 8 + c * 4 + z))
+    return pairs
+
+
+def turned_pairs(pairs):
+    return [(b, a) for a, b in pairs]
+
+
+def paired(
+    inputs,
+    w_query,
+    w_key,
+    w_value,
+    w_gate,
+    w_out,
+    w_act,
+    w_lin,
+    w_down,
+    gain_mix,
+    gain_ffn,
+    cotangent,
+):
+    y, x, c, z = (lax.axis_index(name) for name in ("y", "x", "c", "z"))
+    at = spots_of(x, y, c, z)
+    dk, dv = DK, w_value.shape[2] // 2
+    fence = Fence()
+    link_x, link_y, link_z = (Link(fence, O[k]) for k in ("xd", "yd", "zd"))
+    gains_here = jnp.concatenate(
+        [gain_mix, gain_ffn, jnp.zeros((14, gain_mix.shape[1]), gain_mix.dtype)]
+    )
+    weights = [w_query[0], w_key[0], w_value[0].T, w_gate[0].T, w_out[0]]
+    weights += [w_act[0].T, w_lin[0].T, w_down[0]]
+    mix_rows, ffn_rows, merged, kept = [None] * 4, [None] * 4, [None] * 4, [None] * 4
+
+    def swap_cores(array):
+        return lax.ppermute(array, "c", SWAP)
+
+    def turn_pieces(j, rows, current, over_y):
+        rows[j] = (current, over_y) + tuple(
+            swap_cores(tie(piece, *fence.before)) for piece in (current, over_y)
+        )
+
+    def home_send(block):
+        return link_x.send(block, XCZ, home_pairs())
+
+    spots = [jnp.stack([2 * ((z - j) % 4) + x, x]).astype(jnp.int32) for j in range(4)]
+
+    def mix_forward(j, *after):
+        kept[j] = mix_block(tie(spots[j], *after, *fence.before), normed_in, mix_rows[j], dk, dv)
+        merged[j] = kept[j][-1]
+        return merged[j]
+
+    seq_parts = split_blocks(at, inputs[:, 0])
+    seq_1, seq_3 = link_z.group([(seq_parts[k], XCZ, round_pairs(k)) for k in (1, 3)])
+    mix_own, mix_send, ffn_own, ffn_send = prepare(
+        tie(at, seq_parts[0]), weights, gains_here, dk, dv
+    )
+    mix_start = join(at, mix_own, link_x.swap(mix_send, "x"))
+    fence.close()
+    first = tie(mix_start, *fence.before)
+    over_y = link_y.swap(first, "y")
+    mix_1 = link_z.send(first, "z", RING)
+    ffn_start = join(at, ffn_own, link_x.swap(ffn_send, "x"))
+    other_0 = home_send(seq_parts[0])
+    fence.close()
+    turn_pieces(0, mix_rows, first, over_y)
+    over_y = link_y.swap(ffn_start, "y")
+    seq_2 = link_z.send(seq_parts[2], XCZ, round_pairs(2))
+    other_1 = home_send(seq_1)
+    fence.close()
+    cot_parts = split_blocks(tie(at, *fence.before), cotangent[:, 0])
+    turn_pieces(0, ffn_rows, ffn_start, over_y)
+    over_y = link_y.swap(mix_1, "y")
+    mix_2 = link_z.send(mix_1, "z", RING)
+    other_3, other_2 = home_send(seq_3), home_send(seq_2)
+    gains = jnp.concatenate(
+        [piece[3 * dv + 2 * dk :] for piece in mix_rows[0]], axis=1
+    ).astype(F32)
+    fence.close()
+    turn_pieces(1, mix_rows, mix_1, over_y)
+    over_y = link_y.swap(mix_2, "y")
+    mix_3 = link_z.send(mix_2, "z", RING)
+    cot_other = home_send(cot_parts[0])
+    own_stream, normed_in = assemble(
+        tie(at, *fence.before),
+        (seq_parts[0], seq_1, seq_2, seq_3),
+        (other_0, other_1, other_2, other_3),
+        gains,
+    )
+    half = own_stream.shape[0]
+    fence.now.append(mix_forward(0))
+    fence.close()
+    mix_blocks = {0: mix_start, 1: mix_1, 2: mix_2, 3: mix_3}
+    ffn_blocks = {0: ffn_start}
+    mix_over, ffn_over = {2: over_y}, {}
+    cot_blocks, cot_others = {0: cot_parts[0]}, {0: cot_other}
+    acts, ffn_grads = [[None] * 4, [None] * 4], [None] * 4
+
+    def ffn_sum(first, count, which, kind, *after):
+        sources = list(acts[which])
+        if after:
+            sources[0] = tie(sources[0], *after)
+        return sum_blocks(sources, ffn_rows, first, first, count, None, kind)
+
+    class Scatter:
+        def __init__(self, blocks):
+            self.blocks, self.got, self.ready, self.over, self.running = blocks, {}, {}, {}, None
+            self.passed, self.steps = {}, list(ORDER)
+
+        def turn(self, j):
+            own_0, own_1, send_0, send_1 = self.blocks[j]
+            self.ready[j] = add(own_1, swap_cores(send_1))
+            self.got[j] = (own_0, swap_cores(send_0))
+
+        def cross(self, j, *after):
+            self.over[j] = link_y.swap(self.ready[j], "y", self.got[j][1], *after)
+
+        def pass_on(self, j):
+            assert self.steps.pop(0) == j
+            terms = self.got[j] + (self.over[j],)
+            if self.running is None:
+                self.running = add(*terms)
+            else:
+                self.passed[j] = link_z.send(self.running, "z", RING)
+                self.running = add(self.passed[j], *terms)
+
+    fs = Scatter(ffn_grads)
+    V = {}
+
+    def give_back_x(own_half):
+        parts = own_half.reshape(2, own_half.shape[0] // 2, -1)
+        return link_x.group([(part, XCZ, turned_pairs(home_pairs())) for part in (parts[0], parts[1])])
+
+    def final_swap(block):
+        side = block.shape[1] // 2
+        keep = pick((block[:, :side], block[:, side:]), x)
+        send = pick((block[:, side:], block[:, :side]), x)
+        return keep, link_x.swap(send, "x")
+
+    def gain_totals(*sums):
+        sums, width = jnp.concatenate(sums), gain_mix.shape[1]
+        total = jnp.concatenate(
+            [
+                lax.dynamic_slice_in_dim(sums, width * lax.bitwise_xor(4 * c + 2 * y, p), width, axis=1)
+                for p in (0, 4, 1, 5, 2, 6, 3, 7)
+            ],
+            axis=1,
+        )
+        for axis in ("c", "y", "x"):
+            total = total + lax.ppermute(tie(total, *fence.before), axis, SWAP)
+        fence.now.append(total)
+        return total
+
+    def gain_end(total):
+        total, width = tie(total, *fence.before), gain_mix.shape[1]
+        turned = [
+            lax.ppermute(total, "z", [(i, (i + shift) % 4) for i in range(4)]) for shift in (1, 2, 3)
+        ]
+        fence.now += turned
+        total = total + turned[0] + turned[1] + turned[2]
+        return lax.dynamic_slice_in_dim(total, width * (4 * y + 2 * x + c), width, axis=1)
+
+    count = 2 * dv + 2 * dk
+    token_grads, mix_grads = [None] * 4, [None] * 4
+    ms = Scatter(mix_grads)
+    last = []
+    for step in O["back"]:
+        op, j = step[0], int(step[1:] or 0)
+        after = tuple(last) + fence.before
+        ran = None
+        if op == "|":
+            fence.close()
+        elif op == "h":
+            mix_over[j] = link_y.swap(mix_blocks[j], "y")
+        elif op == "H":
+            ffn_over[j] = link_y.swap(ffn_blocks[j], "y")
+        elif op == "u":
+            turn_pieces(j, mix_rows, mix_blocks[j], mix_over[j])
+        elif op == "U":
+            turn_pieces(j, ffn_rows, ffn_blocks[j], ffn_over[j])
+        elif op == "v":
+            ffn_blocks[j] = link_z.send(ffn_blocks[j - 1], "z", RING)
+        elif op == "r":
+            shifts = ((2,), (1, 3), (1, 2, 3))[j]
+            sends = [(cot_parts[k], XCZ, round_pairs(k)) for k in shifts]
+            cot_blocks.update(zip(shifts, link_z.group(sends)))
+        elif op == "x":
+            cot_others[j] = home_send(cot_blocks[j])
+        elif op == "B":
+            ran = mix_forward(j, *last)
+        elif op == "A":
+            ran = V["A"] = sum_blocks([tie(merged[0], *after)] + merged[1:], mix_rows, 0, 0, dv, 1, BF16)
+        elif op == "D":
+            ran = sum_blocks([tie(merged[0], *after)] + merged[1:], mix_rows, 0, 0, dv, 0, F32)
+            V["D"] = ran
+        elif op == "L":
+            middle, mid_own = middle_block(own_stream, tie(V["D"], *after), V["A"], gains)
+            ran = mid_own
+            mid_sides = (mid_own, link_x.swap(mid_own, "x"))
+        elif op == "W":
+            order = range(4)
+            cot = assemble(
+                tie(at, *after), [cot_blocks[k] for k in order], [cot_others[k] for k in order]
+            )
+            ran = cot
+        elif op in "ef":
+            which = "ef".index(op)
+            acts[which][j] = ffn_block(tie(mid_sides[which], *after), cot, ffn_rows[j], which)
+            ran = acts[which][j]
+        elif op == "s":
+            ran = V["S"] = ffn_sum(0, 2 * dv, 1, BF16, *after)
+        elif op == "g":
+            ffn_grads[j] = ffn_grad_block(mid_sides, cot, (tie(acts[0][j], *after), acts[1][j]))
+            ran = ffn_grads[j][3]
+        elif op == "m":
+            ran = ffn_sum(0, 2 * dv, 0, F32, *after)
+            V["m"] = ran
+        elif op == "n":
+            gain_second, grad_middle, send_own = norm_back_block(
+                1, middle, V["m"], tie(V["S"], *after), cot, gains, (F32, BF16)
+            )
+            send_mix = (send_own, link_x.swap(send_own, "x"))
+            ran = send_own
+        elif op == "o":
+            ran = ffn_sum(2 * dv, dv, 1, BF16, *after)
+            V["q"] = ran
+        elif op == "Q":
+            name = "ASqI"[j]
+            V[name] = link_x.swap(V[name], "x")
+        elif op == "w":
+            ran = ffn_sum(2 * dv, dv, 0, F32, *after)
+            V["w"] = ran
+        elif op == "X":
+            out_own = add(middle, V["w"], V["q"])
+            V["X"] = give_back_x(out_own)
+        elif op in "ZG":
+            if op + "0" not in V:
+                V[op + "0"] = spread_blocks(at, *((out_own, V["X"]) if op == "Z" else (grad_stream, V["K"])))
+            shifts = ((2,), (1, 3), (1, 2, 3))[j]
+            sends = [(V[op + "0"][k], XCZ, turned_pairs(round_pairs(k))) for k in shifts]
+            for k, result in zip(shifts, link_z.group(sends)):
+                V[op, k] = result
+        elif op == "t":
+            fs.turn(j)
+        elif op == "c":
+            fs.cross(j)
+        elif op == "p":
+            fs.pass_on(j)
+        elif op == "T":
+            ms.turn(j)
+        elif op == "C":
+            ms.cross(j)
+        elif op == "P":
+            ms.pass_on(j)
+        elif op == "a":
+            token_grads[j] = mix_back_block(
+                tie(spots[j], *after), send_mix, mix_rows[j], kept[j][:4], dk, dv
+            )
+            ran = token_grads[j]
+        elif op == "b":
+            mix_grads[j] = mix_grad_block(send_mix, normed_in, merged[j], tie(token_grads[j], *after))
+            ran = mix_grads[j][3]
+        elif op == "i":
+            ran = sum_blocks([tie(token_grads[0], *after)] + token_grads[1:], mix_rows, 0, dv, count, 1, BF16)
+            V["I"] = ran
+        elif op == "j":
+            ran = sum_blocks([tie(token_grads[0], *after)] + token_grads[1:], mix_rows, 0, dv, count, 0, F32)
+            V["j"] = ran
+        elif op == "k":
+            gain_first, grad_stream = norm_back_block(
+                0, own_stream, V["j"], tie(V["I"], *after), grad_middle, gains, (BF16,)
+            )
+            V["K"] = give_back_x(grad_stream)
+            ran = grad_stream
+        elif op == "F":
+            assert not fs.steps
+            ffn_end = final_swap(fs.running)
+        elif op == "M":
+            assert not ms.steps
+            mix_end = final_swap(tie(ms.running, V["G0"][0], V["E"]))
+        elif op == "E":
+            if j == 0:
+                V["E"] = gain_totals(gain_first, gain_second)
+            else:
+                mine = gain_end(V["E"])
+        else:
+            raise ValueError(step)
+        if ran is not None:
+            last = [ran]
+            fence.now.append(ran)
+    out_blocks, grad_blocks = ([V[op + "0"][0], V[op, 1], V[op, 2], V[op, 3]] for op in "ZG")
+    output = finish_tokens(at, out_blocks, BF16)
+
+    grad_act, grad_lin, grad_down = finish_rows(
+        at, *ffn_end, ((0, dv), (dv, dv), (2 * dv, dv)), (False,) * 3
+    )
+    grad_out, grad_gate, grad_value, grad_query, grad_key = finish_rows(
+        at,
+        *mix_end,
+        ((0, dv), (dv, dv), (2 * dv, dv), (3 * dv, dk), (3 * dv + dk, dk)),
+        (False, False, False, True, True),
+    )
+    grad_input = finish_tokens(tie(at, grad_act, grad_out, output, mine), grad_blocks, F32)
+    return (
+        output[:, None],
+        grad_input[:, None],
+        grad_query[None],
+        grad_key[None],
+        grad_value.T[None],
+        grad_gate.T[None],
+        grad_out[None],
+        grad_act.T[None],
+        grad_lin.T[None],
+        grad_down[None],
+        mine[:1],
+        mine[1:],
+    )
+
+
+def placed(step, mesh, dp, tensor):
+    tokens, columns = P(None, dp, tensor, None), P(None, dp, tensor)
+    rows, gain = P(None, tensor, dp), P(None, dp)
+    weights = (columns,) * 4 + (rows,) + (columns,) * 2 + (rows,)
+    return jax.shard_map(
+        step,
+        mesh=mesh,
+        in_specs=(tokens,) + weights + (gain, gain, tokens),
+        out_specs=(tokens, tokens) + weights + (gain, gain),
+        check_vma=False,
+    )
+
+
 def solution(mesh):
-    in_specs = (
-        P(None, "dp", "tensor", None),
-        P(None, "dp", "tensor"),
-        P(None, "dp", "tensor"),
-        P(None, "dp", "tensor"),
-        P(None, "dp", "tensor"),
-        P(None, "tensor", "dp"),
-        P(None, "dp", "tensor"),
-        P(None, "dp", "tensor"),
-        P(None, "tensor", "dp"),
-        P(None, "dp"),
-        P(None, "dp"),
-        P(None, "dp", "tensor", None),
-    )
-    out_specs = (
-        P(None, "dp", "tensor", None),
-        P(None, "dp", "tensor", None),
-        P(None, "dp", "tensor"),
-        P(None, "dp", "tensor"),
-        P(None, "dp", "tensor"),
-        P(None, "dp", "tensor"),
-        P(None, "tensor", "dp"),
-        P(None, "dp", "tensor"),
-        P(None, "dp", "tensor"),
-        P(None, "tensor", "dp"),
-        P(None, "dp"),
-        P(None, "dp"),
-    )
-    return jax.shard_map(shards, mesh=mesh, in_specs=in_specs, out_specs=out_specs, check_vma=False)
+    if mesh.shape["dp"] == 8 and mesh.shape["tensor"] == 4:
+        fine = jax.sharding.Mesh(mesh.devices.reshape(2, 2, 2, 4), ("y", "x", "c", "z"))
+        return placed(paired, fine, ("y", "x", "c"), "z")
+    return placed(shards, mesh, "dp", "tensor")

time: 2090 us -> 978 us (0.47)
  waiting for transfers between devices: 1580 us -> 294 us
  Pallas kernels: 0 us -> 437 us
  matrix products: 352 us -> 0 us
  starting transfers between devices: 3.8 us -> 116 us
  blocking collectives: 38.6 us -> 0 us
  local copies, waits for them, and re-layouts: 28.2 us -> 56.6 us
    reduce_scatter x16 -> x0, waiting for transfers between devices: 779 us -> none  [the longest x4 282 us: collect_grads(): lax.psum_scatter(partial_value.astype(jnp.bfloat16), 'tensor', scatter_di...]
    all_gather x16 -> x0, waiting for transfers between devices: 745 us -> none  [the longest x4 296 us: spread_rows(): return lax.all_gather(normed_rows, 'tensor', axis=1, tiled=True)]
    pallas_call x0 -> x48, Pallas kernels: none -> 437 us  [the longest x8 99 us: sum_blocks(): pl.pallas_call(functools.partial(sum_kernel, n, source_first, first, coun...]
    dot_general x60 -> x0, matrix products: 352 us -> none  [the longest x16 107 us: project(): jnp.einsum('bsd,de->bse', in_rows, weight_mat, preferred_element_type=jnp...]
    ppermute x0 -> x101, waiting for transfers between devices: none -> 294 us  [the longest x63 269 us: group(): results.append(lax.ppermute(array, axis, pairs))]
    ppermute x0 -> x101, starting transfers between devices: none -> 116 us  [the longest x63 101 us: group(): results.append(lax.ppermute(array, axis, pairs))]
    unnamed x36 -> x0, waiting for transfers between devices: 52.5 us -> none
    convert_element_type x17 -> x18, other arithmetic: 28.9 us -> 59.7 us  [the longest x17 59.7 us: add(): return total.astype(BF16)]
  transfers between devices with their start and end apart: 34 -> 101, of which waited for: 31 -> 26; matrix products, arithmetic and copies ran while one was open for 20% -> 7% of each run, Pallas kernels for 0% -> 42%
where the time goes in v1:
time: 978 us; the launch traced here: 969 us
  Pallas kernels  437 us (45%)
  waiting for transfers between devices  294 us (30%)
  starting transfers between devices  116 us (12%)
  other arithmetic  62.8 us (6%)
  local copies, waits for them, and re-layouts  56.6 us (6%)
    ppermute x63, waiting for transfers between devices, group(): results.append(lax.ppermute(array, axis, pairs))  269 us
    ppermute x63, starting transfers between devices, group(): results.append(lax.ppermute(array, axis, pairs))  101 us
    pallas_call x8, Pallas kernels, sum_blocks(): pl.pallas_call(functools.partial(sum_kernel, n, source_first, first, coun...  99 us
    pallas_call x8, Pallas kernels, ffn_block(): pl.pallas_call(functools.partial(ffn_kernel, dv, half * tokens), out_shap...  65 us
    convert_element_type x17, other arithmetic, add(): return total.astype(BF16)  59.7 us
    pallas_call x4, Pallas kernels, mix_block(): pl.pallas_call(functools.partial(mix_kernel, dk, dv), out_shape=(shape_of...  59.1 us
    pallas_call x4, Pallas kernels, mix_grad_block(): pl.pallas_call(functools.partial(mix_grad_kernel, dv), out_shape=(out,) *...  54 us
    unnamed x274, local copies, waits for them, and re-layouts  50.6 us
  transfers between devices with their start and end apart: 101, of which 26 were waited for; matrix products, arithmetic and copies ran while one was open for 7% of the time, Pallas kernels for 42%

profile of v1, /device:TPU:0, one launch (start us, length us, event | category | flops | bytes accessed | tf_op | source)
XLA Modules:
  0.0 968.9 jit_solution(13530245375949300501)
XLA Ops:
  17.8 20.9 %collective-permute-done.got = bf16[1824,256]{1,0:T(8,128)(2,1)S(1)} collective-permute-done((bf16[1824,256]{1,0:T(8,128)(2,1)}, bf16[1824,256]{1,0:T(8,128)(2,1)S(1)}, u32[]{:S(2)}, u32[]{:S(2)}) %collective-permute-start) | collective-permute-done | bytes 933920 | tf_op jit(solution)/shard_map/ppermute | solution.py:1006
  43.9 25.4 %collective-permute-done.4.got = bf16[1296,256]{1,0:T(8,128)(2,1)S(1)} collective-permute-done((bf16[1296,256]{1,0:T(8,128)(2,1)S(1)}, bf16[1296,256]{1,0:T(8,128)(2,1)S(1)}, u32[]{:S(2)}, u32[]{:S(2)}) %collective-permute-start.4) | collective-permute-done | bytes 663584 | tf_op jit(solution)/shard_map/ppermute | solution.py:1006
  89.3 19.6 %collective-permute-done.8.refs_2_ = bf16[256,2048]{1,0:T(8,128)(2,1)S(1)} collective-permute-done((bf16[256,2048]{1,0:T(8,128)(2,1)S(1)}, bf16[256,2048]{1,0:T(8,128)(2,1)S(1)}, u32[]{:S(2)}, u32[]{:S(2)}) %collective-permute-start.8) | collective-permute-done | bytes 1048608 | tf_op jit(solution)/shard_map/ppermute | solution.py:1006
  138.3 17.5 %collective-permute-done.10.m1.refs_9_ = bf16[1824,512]{1,0:T(8,128)(2,1)} collective-permute-done((bf16[1824,512]{1,0:T(8,128)(2,1)}, bf16[1824,512]{1,0:T(8,128)(2,1)}, u32[]{:S(2)}, u32[]{:S(2)}) %collective-permute-start.10) | collective-permute-done | bytes 1867808 | tf_op jit(solution)/shard_map/ppermute | solution.py:1006
  186.1 14.7 %mix_block.4 = (bf16[944,1024]{1,0:T(8,128)(2,1)}, f32[432,1024]{1,0:T(8,128)S(1)}, f32[432,1024]{1,0:T(8,128)S(1)}, f32[1,1024]{1,0:T(1,128)S(1)}, bf16[432,1024]{1,0:T(8,128)(2,1)S(1)}) custom-call(s32[2]{0:T(128)S(1)} %pad_add_fusion.1.spots_ref, bf16[1024,2048]{1,0:T(8,128)(2,1)} %get-tuple-element.243.x_ref, bf16[1824,512]{1,0:T(8,128)(2,1)} %copy-done.2, ...), custom_call_target="tpu_custom_call" | custom-call | flops 2164260864 | bytes 5347738 | tf_op jit(solution)/shard_map/mix_block/pallas_call | solution.py:482
  208.3 14.9 %mix_block.5 = (bf16[944,1024]{1,0:T(8,128)(2,1)}, f32[432,1024]{1,0:T(8,128)S(1)}, f32[432,1024]{1,0:T(8,128)S(1)}, f32[1,1024]{1,0:T(1,128)S(1)}, bf16[432,1024]{1,0:T(8,128)(2,1)S(1)}) custom-call(s32[2]{0:T(128)S(1)} %pad_add_fusion.4.spots_ref, bf16[1024,2048]{1,0:T(8,128)(2,1)} %get-tuple-element.243.x_ref, ...), custom_call_target="tpu_custom_call" | custom-call | flops 2164260864 | bytes 5347738 | tf_op jit(solution)/shard_map/mix_block/pallas_call | solution.py:482
  226.5 14.7 %mix_block.6 = (bf16[944,1024]{1,0:T(8,128)(2,1)}, f32[432,1024]{1,0:T(8,128)S(1)}, f32[432,1024]{1,0:T(8,128)S(1)}, f32[1,1024]{1,0:T(1,128)S(1)}, bf16[432,1024]{1,0:T(8,128)(2,1)S(1)}) custom-call(s32[2]{0:T(128)S(1)} %pad_add_fusion.3.spots_ref, bf16[1024,2048]{1,0:T(8,128)(2,1)} %get-tuple-element.243.x_ref, ...), custom_call_target="tpu_custom_call" | custom-call | flops 2164260864 | bytes 5347738 | tf_op jit(solution)/shard_map/mix_block/pallas_call | solution.py:482
  257.9 14.9 %mix_block.7 = (bf16[944,1024]{1,0:T(8,128)(2,1)}, f32[432,1024]{1,0:T(8,128)S(1)}, f32[432,1024]{1,0:T(8,128)S(1)}, f32[1,1024]{1,0:T(1,128)S(1)}, bf16[432,1024]{1,0:T(8,128)(2,1)S(1)}) custom-call(s32[2]{0:T(128)S(1)} %pad_add_fusion.2.spots_ref, bf16[1024,2048]{1,0:T(8,128)(2,1)} %get-tuple-element.243.x_ref, ...), custom_call_target="tpu_custom_call" | custom-call | flops 2164260864 | bytes 5347738 | tf_op jit(solution)/shard_map/mix_block/pallas_call | solution.py:482
  285.7 20.9 %collective-permute-done.31.refs_2_ = bf16[256,2048]{1,0:T(8,128)(2,1)} collective-permute-done((bf16[256,2048]{1,0:T(8,128)(2,1)}, bf16[256,2048]{1,0:T(8,128)(2,1)}, u32[]{:S(2)}, u32[]{:S(2)}) %collective-permute-start.31) | collective-permute-done | bytes 1048608 | tf_op jit(solution)/shard_map/ppermute | solution.py:1006
  307.8 30.5 %collective-permute-done.35.refs_5_ = bf16[256,2048]{1,0:T(8,128)(2,1)S(1)} collective-permute-done((bf16[256,2048]{1,0:T(8,128)(2,1)}, bf16[256,2048]{1,0:T(8,128)(2,1)S(1)}, u32[]{:S(2)}, u32[]{:S(2)}) %collective-permute-start.35) | collective-permute-done | bytes 1048608 | tf_op jit(solution)/shard_map/ppermute | solution.py:1006
  363.6 20.3 %collective-permute-done.42.f0.refs_16_ = bf16[1296,512]{1,0:T(8,128)(2,1)S(1)} collective-permute-done((bf16[1296,512]{1,0:T(8,128)(2,1)S(1)}, bf16[1296,512]{1,0:T(8,128)(2,1)S(1)}, u32[]{:S(2)}, u32[]{:S(2)}) %collective-permute-start.42) | collective-permute-done | bytes 1327136 | tf_op jit(solution)/shard_map/ppermute | solution.py:1006
  449.4 13.1 %sum_blocks.10 = bf16[512,2048]{1,0:T(8,128)(2,1)} custom-call(bf16[1296,512]{1,0:T(8,128)(2,1)S(1)} %ffn_block.11.refs_0_.a1, bf16[1296,512]{1,0:T(8,128)(2,1)S(1)} %copy-done.29, bf16[1296,512]{1,0:T(8,128)(2,1)S(1)} %ffn_block.12.refs_2_.a1, bf16[1296,512]{1,0:T(8,128)(2,1)S(1)} %ffn_block.13.refs_3_.a1, bf16[1296,512]{1,0:T(8,128)(2,1)} %copy-done.10, ...), custom_call_target="tpu_custom_call" | custom-call | flops 2174327296 | bytes 6566708 | tf_op jit(solution)/shard_map/sum_blocks/pallas_call | solution.py:648
  505.4 13.6 %sum_blocks.11.partial = f32[512,2048]{1,0:T(8,128)} custom-call(bf16[1296,512]{1,0:T(8,128)(2,1)S(1)} %copy-done.24, bf16[1296,512]{1,0:T(8,128)(2,1)S(1)} %copy-done.27, bf16[1296,512]{1,0:T(8,128)(2,1)S(1)} %copy-done.34, bf16[1296,512]{1,0:T(8,128)(2,1)S(1)} %ffn_block.15.refs_3_.a0, bf16[1296,512]{1,0:T(8,128)(2,1)} %copy-done.10, ...), custom_call_target="tpu_custom_call" | custom-call | flops 2174327296 | bytes 6566708 | tf_op jit(solution)/shard_map/sum_blocks/pallas_call | solution.py:648
  594.5 12.8 %mix_back_block.4.grad_ref.refs_1_ = bf16[1376,1024]{1,0:T(8,128)(2,1)} custom-call(s32[2]{0:T(128)S(1)} %pad_add_fusion.4.spots_ref, bf16[512,2048]{1,0:T(8,128)(2,1)} %copy-done, bf16[512,2048]{1,0:T(8,128)(2,1)} %collective-permute-done.51.s1, bf16[1824,512]{1,0:T(8,128)(2,1)} %collective-permute-done.3.m0.refs_8_, ...), custom_call_target="tpu_custom_call" | custom-call | flops 1570347392 | bytes 5033165 | tf_op jit(solution)/shard_map/mix_back_block/pallas_call | solution.py:554
  607.3 13.5 %mix_grad_block.4 = (bf16[1808,512]{1,0:T(8,128)(2,1)S(1)}, bf16[1808,512]{1,0:T(8,128)(2,1)S(1)}, bf16[1808,512]{1,0:T(8,128)(2,1)}, bf16[1808,512]{1,0:T(8,128)(2,1)}) custom-call(bf16[512,2048]{1,0:T(8,128)(2,1)} %copy-done, bf16[512,2048]{1,0:T(8,128)(2,1)} %collective-permute-done.51.s1, bf16[1024,2048]{1,0:T(8,128)(2,1)} %get-tuple-element.243.x_ref, ...), custom_call_target="tpu_custom_call" | custom-call | flops 2274990592 | bytes 6291457 | tf_op jit(solution)/shard_map/mix_grad_block/pallas_call | solution.py:594
  664.0 13.3 %mix_grad_block.5 = (bf16[1808,512]{1,0:T(8,128)(2,1)S(1)}, bf16[1808,512]{1,0:T(8,128)(2,1)S(1)}, bf16[1808,512]{1,0:T(8,128)(2,1)}, bf16[1808,512]{1,0:T(8,128)(2,1)}) custom-call(bf16[512,2048]{1,0:T(8,128)(2,1)} %copy-done, bf16[512,2048]{1,0:T(8,128)(2,1)} %collective-permute-done.51.s1, bf16[1024,2048]{1,0:T(8,128)(2,1)} %get-tuple-element.243.x_ref, ...), custom_call_target="tpu_custom_call" | custom-call | flops 2274990592 | bytes 6291457 | tf_op jit(solution)/shard_map/mix_grad_block/pallas_call | solution.py:594
  715.8 12.8 %mix_back_block.6.grad_ref.refs_3_ = bf16[1376,1024]{1,0:T(8,128)(2,1)} custom-call(s32[2]{0:T(128)S(1)} %pad_add_fusion.2.spots_ref, bf16[512,2048]{1,0:T(8,128)(2,1)} %copy-done, bf16[512,2048]{1,0:T(8,128)(2,1)} %collective-permute-done.51.s1, bf16[1824,512]{1,0:T(8,128)(2,1)} %collective-permute-done.17.m0.refs_16_, ...), custom_call_target="tpu_custom_call" | custom-call | flops 1570347392 | bytes 5033165 | tf_op jit(solution)/shard_map/mix_back_block/pallas_call | solution.py:554
  741.0 13.4 %mix_grad_block.6 = (bf16[1808,512]{1,0:T(8,128)(2,1)S(1)}, bf16[1808,512]{1,0:T(8,128)(2,1)S(1)}, bf16[1808,512]{1,0:T(8,128)(2,1)}, bf16[1808,512]{1,0:T(8,128)(2,1)}) custom-call(bf16[512,2048]{1,0:T(8,128)(2,1)} %copy-done, bf16[512,2048]{1,0:T(8,128)(2,1)} %collective-permute-done.51.s1, bf16[1024,2048]{1,0:T(8,128)(2,1)} %get-tuple-element.243.x_ref, ...), custom_call_target="tpu_custom_call" | custom-call | flops 2274990592 | bytes 6291457 | tf_op jit(solution)/shard_map/mix_grad_block/pallas_call | solution.py:594
  762.8 18.1 %sum_blocks.14 = bf16[512,2048]{1,0:T(8,128)(2,1)} custom-call(bf16[1376,1024]{1,0:T(8,128)(2,1)} %mix_back_block.7.refs_0_.grad_ref, bf16[1376,1024]{1,0:T(8,128)(2,1)} %mix_back_block.4.grad_ref.refs_1_, bf16[1376,1024]{1,0:T(8,128)(2,1)} %mix_back_block.5.grad_ref.refs_2_, bf16[1376,1024]{1,0:T(8,128)(2,1)} %mix_back_block.6.grad_ref.refs_3_, ...), custom_call_target="tpu_custom_call" | custom-call | flops 3462817280 | bytes 9712436 | tf_op jit(solution)/shard_map/sum_blocks/pallas_call | solution.py:648
  780.9 13.8 %mix_grad_block.7 = (bf16[1808,512]{1,0:T(8,128)(2,1)S(1)}, bf16[1808,512]{1,0:T(8,128)(2,1)S(1)}, bf16[1808,512]{1,0:T(8,128)(2,1)}, bf16[1808,512]{1,0:T(8,128)(2,1)}) custom-call(bf16[512,2048]{1,0:T(8,128)(2,1)} %copy-done, bf16[512,2048]{1,0:T(8,128)(2,1)} %collective-permute-done.51.s1, bf16[1024,2048]{1,0:T(8,128)(2,1)} %get-tuple-element.243.x_ref, ...), custom_call_target="tpu_custom_call" | custom-call | flops 2274990592 | bytes 6291457 | tf_op jit(solution)/shard_map/mix_grad_block/pallas_call | solution.py:594
  815.1 18.9 %sum_blocks.15.partial = f32[512,2048]{1,0:T(8,128)} custom-call(bf16[1376,1024]{1,0:T(8,128)(2,1)} %mix_back_block.7.refs_0_.grad_ref, bf16[1376,1024]{1,0:T(8,128)(2,1)} %mix_back_block.4.grad_ref.refs_1_, bf16[1376,1024]{1,0:T(8,128)(2,1)} %mix_back_block.5.grad_ref.refs_2_, bf16[1376,1024]{1,0:T(8,128)(2,1)} %mix_back_block.6.grad_ref.refs_3_, ...), custom_call_target="tpu_custom_call" | custom-call | flops 3462817280 | bytes 9712436 | tf_op jit(solution)/shard_map/sum_blocks/pallas_call | solution.py:648
  837.5 15.3 %collective-permute-done.83 = bf16[1808,512]{1,0:T(8,128)(2,1)} collective-permute-done((bf16[1808,512]{1,0:T(8,128)(2,1)}, bf16[1808,512]{1,0:T(8,128)(2,1)}, u32[]{:S(2)}, u32[]{:S(2)}) %collective-permute-start.83) | collective-permute-done | bytes 1851424 | tf_op jit(solution)/shard_map/ppermute | solution.py:1006
  874.4 23.6 %collective-permute-done.92 = f32[2,2048]{1,0:T(2,128)S(1)} collective-permute-done((f32[2,2048]{1,0:T(2,128)S(1)}, f32[2,2048]{1,0:T(2,128)S(1)}, u32[]{:S(2)}, u32[]{:S(2)}) %collective-permute-start.92) | collective-permute-done | bytes 16416 | tf_op jit(solution)/shard_map/ppermute | solution.py:1194
  934.6 24.1 %collective-permute-done.82.got = bf16[1296,256]{1,0:T(8,128)(2,1)S(1)} collective-permute-done((bf16[1296,256]{1,0:T(8,128)(2,1)}, bf16[1296,256]{1,0:T(8,128)(2,1)S(1)}, u32[]{:S(2)}, u32[]{:S(2)}) %collective-permute-start.82) | collective-permute-done | bytes 663584 | tf_op jit(solution)/shard_map/ppermute | solution.py:1006
  (547 shorter events, 545.9 us)
Async XLA Ops:
  120.9 47.5 %collective-permute-start.14 = (bf16[1824,512]{1,0:T(8,128)(2,1)S(1)}, bf16[1824,512]{1,0:T(8,128)(2,1)S(1)}, u32[]{:S(2)}, u32[]{:S(2)}) collective-permute-start(bf16[1824,512]{1,0:T(8,128)(2,1)S(1)} %join.2.m0.refs_4_), channel_id=1, source_target_pairs={{0,4},{4,0},{1,5},{5,1},{2,6},{6,2},{3,7},{7,3},{8,12},{12,8},{9,1... | collective-permute-start | bytes 5603336 | tf_op jit(solution)/shard_map/ppermute | solution.py:1080
  254.2 52.4 %collective-permute-start.30 = (bf16[1296,512]{1,0:T(8,128)(2,1)S(1)}, bf16[1296,512]{1,0:T(8,128)(2,1)}, u32[]{:S(2)}, u32[]{:S(2)}) collective-permute-start(bf16[1296,512]{1,0:T(8,128)(2,1)S(1)} %join.3.f0.refs_4_), channel_id=1, source_target_pairs={{0,1},{1,2},{2,3},{3,0},{4,5},{5,6},{6,7},{7,4},{8,9},{9,10},{10,1... | collective-permute-start | bytes 3981320 | tf_op jit(solution)/shard_map/ppermute | solution.py:1006
  254.2 52.4 %collective-permute-start.33 = (bf16[1296,512]{1,0:T(8,128)(2,1)S(1)}, bf16[1296,512]{1,0:T(8,128)(2,1)}, u32[]{:S(2)}, u32[]{:S(2)}) collective-permute-start(bf16[1296,512]{1,0:T(8,128)(2,1)S(1)} %join.3.f0.refs_4_), channel_id=1, source_target_pairs={{0,16},{16,0},{1,17},{17,1},{2,18},{18,2},{3,19},{19,3},{4,20},{20... | collective-permute-start | bytes 3981320 | tf_op jit(solution)/shard_map/ppermute | solution.py:1006
  255.7 50.9 %collective-permute-start.31 = (bf16[256,2048]{1,0:T(8,128)(2,1)}, bf16[256,2048]{1,0:T(8,128)(2,1)}, u32[]{:S(2)}, u32[]{:S(2)}) collective-permute-start(bf16[256,2048]{1,0:T(8,128)(2,1)} %copy-done.118), channel_id=1, source_target_pairs={{2,0},{0,2},{7,5},{5,7},{11,9},{9,11},{14,12},{12,14},{18,16},{16,... | collective-permute-start | bytes 3145736 | tf_op jit(solution)/shard_map/ppermute | solution.py:1006
  281.7 70.4 %collective-permute-start.29 = (bf16[512,2048]{1,0:T(8,128)(2,1)}, bf16[512,2048]{1,0:T(8,128)(2,1)}, u32[]{:S(2)}, u32[]{:S(2)}) collective-permute-start(bf16[512,2048]{1,0:T(8,128)(2,1)} %sum_blocks.8), channel_id=1, source_target_pairs={{0,8},{8,0},{1,9},{9,1},{2,10},{10,2},{3,11},{11,3},{4,12},{12,4},... | collective-permute-start | bytes 6291464 | tf_op jit(solution)/shard_map/ppermute | solution.py:1006
  281.8 56.5 %collective-permute-start.35 = (bf16[256,2048]{1,0:T(8,128)(2,1)}, bf16[256,2048]{1,0:T(8,128)(2,1)S(1)}, u32[]{:S(2)}, u32[]{:S(2)}) collective-permute-start(bf16[256,2048]{1,0:T(8,128)(2,1)} %collective-permute-done.24.refs_1_), channel_id=1, source_target_pairs={{0,8},{9,1},{2,10},{11,3},{12,4},{5,13},{14,6},{7,15},{16,24},{25,... | collective-permute-start | bytes 3145736 | tf_op jit(solution)/shard_map/ppermute | solution.py:1006
  361.5 51.0 %collective-permute-start.39 = (bf16[512,2048]{1,0:T(8,128)(2,1)S(1)}, bf16[512,2048]{1,0:T(8,128)(2,1)}, u32[]{:S(2)}, u32[]{:S(2)}) collective-permute-start(bf16[512,2048]{1,0:T(8,128)(2,1)S(1)} %get-tuple-element.305.x_ref.x0), channel_id=1, source_target_pairs={{0,8},{8,0},{1,9},{9,1},{2,10},{10,2},{3,11},{11,3},{4,12},{12,4},... | collective-permute-start | bytes 6291464 | tf_op jit(solution)/shard_map/ppermute | solution.py:1006
  462.5 59.3 %collective-permute-start.49 = (bf16[512,2048]{1,0:T(8,128)(2,1)}, bf16[512,2048]{1,0:T(8,128)(2,1)S(1)}, u32[]{:S(2)}, u32[]{:S(2)}) collective-permute-start(bf16[512,2048]{1,0:T(8,128)(2,1)} %sum_blocks.10), channel_id=1, source_target_pairs={{0,8},{8,0},{1,9},{9,1},{2,10},{10,2},{3,11},{11,3},{4,12},{12,4},... | collective-permute-start | bytes 6291464 | tf_op jit(solution)/shard_map/ppermute | solution.py:1006
  505.3 55.3 %collective-permute-start.59 = (bf16[1296,512]{1,0:T(8,128)(2,1)}, bf16[1296,512]{1,0:T(8,128)(2,1)}, u32[]{:S(2)}, u32[]{:S(2)}) collective-permute-start(bf16[1296,512]{1,0:T(8,128)(2,1)} %get-tuple-element.307), channel_id=1, source_target_pairs={{0,4},{4,0},{1,5},{5,1},{2,6},{6,2},{3,7},{7,3},{8,12},{12,8},{9,1... | collective-permute-start | bytes 3981320 | tf_op jit(solution)/shard_map/ppermute | solution.py:1080
  521.8 60.5 %collective-permute-start.56 = (bf16[1296,512]{1,0:T(8,128)(2,1)}, bf16[1296,512]{1,0:T(8,128)(2,1)}, u32[]{:S(2)}, u32[]{:S(2)}) collective-permute-start(bf16[1296,512]{1,0:T(8,128)(2,1)} %add_convert_fusion.16), channel_id=1, source_target_pairs={{0,16},{16,0},{1,17},{17,1},{2,18},{18,2},{3,19},{19,3},{4,20},{20... | collective-permute-start | bytes 3981320 | tf_op jit(solution)/shard_map/ppermute | solution.py:1006
  522.8 64.1 %collective-permute-start.58 = (bf16[1296,512]{1,0:T(8,128)(2,1)}, bf16[1296,512]{1,0:T(8,128)(2,1)}, u32[]{:S(2)}, u32[]{:S(2)}) collective-permute-start(bf16[1296,512]{1,0:T(8,128)(2,1)} %get-tuple-element.330), channel_id=1, source_target_pairs={{0,4},{4,0},{1,5},{5,1},{2,6},{6,2},{3,7},{7,3},{8,12},{12,8},{9,1... | collective-permute-start | bytes 3981320 | tf_op jit(solution)/shard_map/ppermute | solution.py:1080
  533.3 60.7 %collective-permute-start.51 = (bf16[512,2048]{1,0:T(8,128)(2,1)S(1)}, bf16[512,2048]{1,0:T(8,128)(2,1)}, u32[]{:S(2)}, u32[]{:S(2)}) collective-permute-start(bf16[512,2048]{1,0:T(8,128)(2,1)S(1)} %get-tuple-element.319.s0), channel_id=1, source_target_pairs={{0,8},{8,0},{1,9},{9,1},{2,10},{10,2},{3,11},{11,3},{4,12},{12,4},... | collective-permute-start | bytes 6291464 | tf_op jit(solution)/shard_map/ppermute | solution.py:1006
  582.3 48.0 %collective-permute-start.50 = (bf16[512,2048]{1,0:T(8,128)(2,1)}, bf16[512,2048]{1,0:T(8,128)(2,1)}, u32[]{:S(2)}, u32[]{:S(2)}) collective-permute-start(bf16[512,2048]{1,0:T(8,128)(2,1)} %sum_blocks.12), channel_id=1, source_target_pairs={{0,8},{8,0},{1,9},{9,1},{2,10},{10,2},{3,11},{11,3},{4,12},{12,4},... | collective-permute-start | bytes 6291464 | tf_op jit(solution)/shard_map/ppermute | solution.py:1006
  594.0 68.7 %collective-permute-start.66 = (bf16[1296,512]{1,0:T(8,128)(2,1)S(1)}, bf16[1296,512]{1,0:T(8,128)(2,1)}, u32[]{:S(2)}, u32[]{:S(2)}) collective-permute-start(bf16[1296,512]{1,0:T(8,128)(2,1)S(1)} %copy-done.116), channel_id=1, source_target_pairs={{0,4},{4,0},{1,5},{5,1},{2,6},{6,2},{3,7},{7,3},{8,12},{12,8},{9,1... | collective-permute-start | bytes 3981320 | tf_op jit(solution)/shard_map/ppermute | solution.py:1080
  620.8 56.6 %collective-permute-start.72 = (bf16[1808,512]{1,0:T(8,128)(2,1)}, bf16[1808,512]{1,0:T(8,128)(2,1)}, u32[]{:S(2)}, u32[]{:S(2)}) collective-permute-start(bf16[1808,512]{1,0:T(8,128)(2,1)} %get-tuple-element.340), channel_id=1, source_target_pairs={{0,4},{4,0},{1,5},{5,1},{2,6},{6,2},{3,7},{7,3},{8,12},{12,8},{9,1... | collective-permute-start | bytes 5554184 | tf_op jit(solution)/shard_map/ppermute | solution.py:1080
  696.9 58.8 %collective-permute-start.74 = (bf16[1808,512]{1,0:T(8,128)(2,1)}, bf16[1808,512]{1,0:T(8,128)(2,1)}, u32[]{:S(2)}, u32[]{:S(2)}) collective-permute-start(bf16[1808,512]{1,0:T(8,128)(2,1)} %add_convert_fusion.8), channel_id=1, source_target_pairs={{0,16},{16,0},{1,17},{17,1},{2,18},{18,2},{3,19},{19,3},{4,20},{20... | collective-permute-start | bytes 5554184 | tf_op jit(solution)/shard_map/ppermute | solution.py:1006
  698.0 61.9 %collective-permute-start.76 = (bf16[1808,512]{1,0:T(8,128)(2,1)}, bf16[1808,512]{1,0:T(8,128)(2,1)}, u32[]{:S(2)}, u32[]{:S(2)}) collective-permute-start(bf16[1808,512]{1,0:T(8,128)(2,1)} %get-tuple-element.381), channel_id=1, source_target_pairs={{0,4},{4,0},{1,5},{5,1},{2,6},{6,2},{3,7},{7,3},{8,12},{12,8},{9,1... | collective-permute-start | bytes 5554184 | tf_op jit(solution)/shard_map/ppermute | solution.py:1080
  706.8 52.6 %collective-permute-start.69 = (bf16[256,2048]{1,0:T(8,128)(2,1)}, bf16[256,2048]{1,0:T(8,128)(2,1)}, u32[]{:S(2)}, u32[]{:S(2)}) collective-permute-start(bf16[256,2048]{1,0:T(8,128)(2,1)} %get-tuple-element.356), channel_id=1, source_target_pairs={{0,1},{2,3},{5,6},{7,4},{9,10},{11,8},{12,13},{14,15},{16,17},{18,... | collective-permute-start | bytes 3145736 | tf_op jit(solution)/shard_map/ppermute | solution.py:1006
  709.8 50.1 %collective-permute-start.70 = (bf16[256,2048]{1,0:T(8,128)(2,1)}, bf16[256,2048]{1,0:T(8,128)(2,1)}, u32[]{:S(2)}, u32[]{:S(2)}) collective-permute-start(bf16[256,2048]{1,0:T(8,128)(2,1)} %get-tuple-element.358), channel_id=1, source_target_pairs={{0,2},{2,0},{5,7},{7,5},{9,11},{11,9},{12,14},{14,12},{16,18},{18,... | collective-permute-start | bytes 3145736 | tf_op jit(solution)/shard_map/ppermute | solution.py:1006
  810.9 47.2 %collective-permute-start.79 = (bf16[512,2048]{1,0:T(8,128)(2,1)}, bf16[512,2048]{1,0:T(8,128)(2,1)}, u32[]{:S(2)}, u32[]{:S(2)}) collective-permute-start(bf16[512,2048]{1,0:T(8,128)(2,1)} %sum_blocks.14), channel_id=1, source_target_pairs={{0,8},{8,0},{1,9},{9,1},{2,10},{10,2},{3,11},{11,3},{4,12},{12,4},... | collective-permute-start | bytes 6291464 | tf_op jit(solution)/shard_map/ppermute | solution.py:1006
  857.2 54.2 %collective-permute-start.87 = (bf16[1808,512]{1,0:T(8,128)(2,1)}, bf16[1808,512]{1,0:T(8,128)(2,1)}, u32[]{:S(2)}, u32[]{:S(2)}) collective-permute-start(bf16[1808,512]{1,0:T(8,128)(2,1)} %add_convert_fusion.3), channel_id=1, source_target_pairs={{0,1},{1,2},{2,3},{3,0},{4,5},{5,6},{6,7},{7,4},{8,9},{9,10},{10,1... | collective-permute-start | bytes 5554184 | tf_op jit(solution)/shard_map/ppermute | solution.py:1006
  857.2 60.3 %collective-permute-start.90 = (bf16[1808,512]{1,0:T(8,128)(2,1)}, bf16[1808,512]{1,0:T(8,128)(2,1)}, u32[]{:S(2)}, u32[]{:S(2)}) collective-permute-start(bf16[1808,512]{1,0:T(8,128)(2,1)} %add_convert_fusion.2), channel_id=1, source_target_pairs={{0,16},{16,0},{1,17},{17,1},{2,18},{18,2},{3,19},{19,3},{4,20},{20... | collective-permute-start | bytes 5554184 | tf_op jit(solution)/shard_map/ppermute | solution.py:1006
  911.4 52.9 %collective-permute-start.100 = (bf16[256,2048]{1,0:T(8,128)(2,1)}, bf16[256,2048]{1,0:T(8,128)(2,1)}, u32[]{:S(2)}, u32[]{:S(2)}) collective-permute-start(bf16[256,2048]{1,0:T(8,128)(2,1)} %get-tuple-element.417), channel_id=1, source_target_pairs={{0,3},{2,1},{5,4},{7,6},{9,8},{11,10},{12,15},{14,13},{16,19},{18,... | collective-permute-start | bytes 3145736 | tf_op jit(solution)/shard_map/ppermute | solution.py:1006
  917.5 46.8 %collective-permute-start.99 = (bf16[256,2048]{1,0:T(8,128)(2,1)}, bf16[256,2048]{1,0:T(8,128)(2,1)}, u32[]{:S(2)}, u32[]{:S(2)}) collective-permute-start(bf16[256,2048]{1,0:T(8,128)(2,1)} %get-tuple-element.415), channel_id=1, source_target_pairs={{0,2},{2,0},{5,7},{7,5},{9,11},{11,9},{12,14},{14,12},{16,18},{18,... | collective-permute-start | bytes 3145736 | tf_op jit(solution)/shard_map/ppermute | solution.py:1006
  (214 other events, 4017.6 us)

commit v2 on v1

--- a/solution.py
+++ b/solution.py
@@ -913,7 +913,7 @@
     )(at, mine, got)
 
 
-O = {'xd': 2, 'yd': 1, 'zd': 2, 'scale': 0.3, 'back': ['B1', 'h3', 'r1', 'u2', 'B2', '|', 'r0', 'x1', 'v1', 'H0', 'x3', 'x2', 'u3', 'B3', 'A', '|', '|', 'Q0', 'v2', 'H1', 'D', '|', 'v3', 'H2', 'L', 'U0', 'U1', 'W', 'e0', 'e1', 'H3', 'f1', 'f0', 'U2', '|', 'f2', 'U3', 'f3', 's', '|', 'Q1', 'e2', 'g1', 't1', 'e3', 'g2', 'm', '|', 't2', 'c1', 'p1', 'c2', 'p2', 'n', 'g3', 't3', 'g0', 't0', 'o', 'c3', '|', '|', 'Q2', 'w', 'p3', 'a1', 'b1', 'T1', 'X', 'c0', 'a2', 'p0', 'b2', 'T2', '|', 'C1', 'Z2', 'a3', 'a0', 'b3', 'T3', '|', 'C2', 'P1', 'P2', 'i', 'b0', 'T0', '|', 'C3', 'P3', 'Q3', 'j', 'k', 'C0', '|', '|', 'G2', 'E0', 'P0', 'M', 'F', 'E1']}
+O = {'xd': 2, 'yd': 1, 'zd': 2, 'scale': 0.3, 'back': ['B1', 'h3', 'r1', 'u2', 'B2', '|', 'r0', 'x1', 'v1', 'H0', 'x3', 'u3', 'B3', 'A', '|', '|', 'Q0', 'x2', 'v2', 'H1', 'D', '|', 'v3', 'H2', 'L', 'U0', 'U1', 'W', 'e0', 'e1', 'H3', 'f1', 'U2', '|', 'f0', 'f2', 'U3', 'f3', 's', '|', 'Q1', 'e2', 'g1', 't1', 'e3', 'g2', 'm', '|', 't2', 'c1', 'p1', 'c2', 'p2', 'n', 'g3', 't3', 'g0', 't0', 'o', 'c3', '|', '|', 'Q2', 'w', 'p3', 'a1', 'b1', 'T1', 'X', 'c0', 'a2', 'p0', 'b2', 'T2', '|', 'C1', 'Z2', 'a3', 'a0', 'b3', 'T3', '|', 'C2', 'P1', 'P2', 'i', 'b0', 'T0', '|', 'C3', 'P3', 'Q3', 'j', 'k', 'C0', '|', '|', 'G2', 'E0', 'P0', 'M', 'F', 'E1']}
 
 
 SWAP = ((0, 1), (1, 0))

time: 978 us -> 971 us (level)
    unnamed x274 -> x284, local copies, waits for them, and re-layouts: 50.6 us -> 52.7 us
  transfers between devices with their start and end apart: 101 -> 101, of which waited for: 26 -> 27; matrix products, arithmetic and copies ran while one was open for 7% -> 7% of each run, Pallas kernels for 42% -> 43%
where the time goes in v2:
time: 971 us; the launch traced here: 962 us
  Pallas kernels  437 us (45%)
  waiting for transfers between devices  289 us (30%)
  starting transfers between devices  112 us (12%)
  other arithmetic  62.8 us (6%)
  local copies, waits for them, and re-layouts  58.7 us (6%)
    ppermute x63, waiting for transfers between devices, group(): results.append(lax.ppermute(array, axis, pairs))  265 us
    pallas_call x8, Pallas kernels, sum_blocks(): pl.pallas_call(functools.partial(sum_kernel, n, source_first, first, coun...  99.1 us
    ppermute x63, starting transfers between devices, group(): results.append(lax.ppermute(array, axis, pairs))  95.6 us
    pallas_call x8, Pallas kernels, ffn_block(): pl.pallas_call(functools.partial(ffn_kernel, dv, half * tokens), out_shap...  65.3 us
    convert_element_type x17, other arithmetic, add(): return total.astype(BF16)  59.7 us
    pallas_call x4, Pallas kernels, mix_block(): pl.pallas_call(functools.partial(mix_kernel, dk, dv), out_shape=(shape_of...  59.1 us
    pallas_call x4, Pallas kernels, mix_grad_block(): pl.pallas_call(functools.partial(mix_grad_kernel, dv), out_shape=(out,) *...  54.1 us
    unnamed x284, local copies, waits for them, and re-layouts  52.7 us
  transfers between devices with their start and end apart: 101, of which 27 were waited for; matrix products, arithmetic and copies ran while one was open for 7% of the time, Pallas kernels for 43%

profile of v2, /device:TPU:0, one launch (start us, length us, event | category | flops | bytes accessed | tf_op | source)
XLA Modules:
  0.0 961.6 jit_solution(1651017291520861022)
XLA Ops:
  17.8 20.9 %collective-permute-done.got = bf16[1824,256]{1,0:T(8,128)(2,1)S(1)} collective-permute-done((bf16[1824,256]{1,0:T(8,128)(2,1)}, bf16[1824,256]{1,0:T(8,128)(2,1)S(1)}, u32[]{:S(2)}, u32[]{:S(2)}) %collective-permute-start) | collective-permute-done | bytes 933920 | tf_op jit(solution)/shard_map/ppermute | solution.py:1006
  43.9 25.4 %collective-permute-done.4.got = bf16[1296,256]{1,0:T(8,128)(2,1)S(1)} collective-permute-done((bf16[1296,256]{1,0:T(8,128)(2,1)S(1)}, bf16[1296,256]{1,0:T(8,128)(2,1)S(1)}, u32[]{:S(2)}, u32[]{:S(2)}) %collective-permute-start.4) | collective-permute-done | bytes 663584 | tf_op jit(solution)/shard_map/ppermute | solution.py:1006
  89.3 19.6 %collective-permute-done.8.refs_2_ = bf16[256,2048]{1,0:T(8,128)(2,1)S(1)} collective-permute-done((bf16[256,2048]{1,0:T(8,128)(2,1)S(1)}, bf16[256,2048]{1,0:T(8,128)(2,1)S(1)}, u32[]{:S(2)}, u32[]{:S(2)}) %collective-permute-start.8) | collective-permute-done | bytes 1048608 | tf_op jit(solution)/shard_map/ppermute | solution.py:1006
  138.3 17.5 %collective-permute-done.10.m1.refs_9_ = bf16[1824,512]{1,0:T(8,128)(2,1)} collective-permute-done((bf16[1824,512]{1,0:T(8,128)(2,1)}, bf16[1824,512]{1,0:T(8,128)(2,1)}, u32[]{:S(2)}, u32[]{:S(2)}) %collective-permute-start.10) | collective-permute-done | bytes 1867808 | tf_op jit(solution)/shard_map/ppermute | solution.py:1006
  186.1 14.7 %mix_block.4 = (bf16[944,1024]{1,0:T(8,128)(2,1)}, f32[432,1024]{1,0:T(8,128)S(1)}, f32[432,1024]{1,0:T(8,128)S(1)}, f32[1,1024]{1,0:T(1,128)S(1)}, bf16[432,1024]{1,0:T(8,128)(2,1)S(1)}) custom-call(s32[2]{0:T(128)S(1)} %pad_add_fusion.1.spots_ref, bf16[1024,2048]{1,0:T(8,128)(2,1)} %get-tuple-element.243.x_ref, bf16[1824,512]{1,0:T(8,128)(2,1)} %copy-done.2, ...), custom_call_target="tpu_custom_call" | custom-call | flops 2164260864 | bytes 5347738 | tf_op jit(solution)/shard_map/mix_block/pallas_call | solution.py:482
  208.2 14.9 %mix_block.5 = (bf16[944,1024]{1,0:T(8,128)(2,1)}, f32[432,1024]{1,0:T(8,128)S(1)}, f32[432,1024]{1,0:T(8,128)S(1)}, f32[1,1024]{1,0:T(1,128)S(1)}, bf16[432,1024]{1,0:T(8,128)(2,1)S(1)}) custom-call(s32[2]{0:T(128)S(1)} %pad_add_fusion.4.spots_ref, bf16[1024,2048]{1,0:T(8,128)(2,1)} %get-tuple-element.243.x_ref, ...), custom_call_target="tpu_custom_call" | custom-call | flops 2164260864 | bytes 5347738 | tf_op jit(solution)/shard_map/mix_block/pallas_call | solution.py:482
  226.5 14.7 %mix_block.6 = (bf16[944,1024]{1,0:T(8,128)(2,1)}, f32[432,1024]{1,0:T(8,128)S(1)}, f32[432,1024]{1,0:T(8,128)S(1)}, f32[1,1024]{1,0:T(1,128)S(1)}, bf16[432,1024]{1,0:T(8,128)(2,1)S(1)}) custom-call(s32[2]{0:T(128)S(1)} %pad_add_fusion.3.spots_ref, bf16[1024,2048]{1,0:T(8,128)(2,1)} %get-tuple-element.243.x_ref, ...), custom_call_target="tpu_custom_call" | custom-call | flops 2164260864 | bytes 5347738 | tf_op jit(solution)/shard_map/mix_block/pallas_call | solution.py:482
  259.6 14.9 %mix_block.7 = (bf16[944,1024]{1,0:T(8,128)(2,1)}, f32[432,1024]{1,0:T(8,128)S(1)}, f32[432,1024]{1,0:T(8,128)S(1)}, f32[1,1024]{1,0:T(1,128)S(1)}, bf16[432,1024]{1,0:T(8,128)(2,1)S(1)}) custom-call(s32[2]{0:T(128)S(1)} %pad_add_fusion.2.spots_ref, bf16[1024,2048]{1,0:T(8,128)(2,1)} %get-tuple-element.243.x_ref, ...), custom_call_target="tpu_custom_call" | custom-call | flops 2164260864 | bytes 5347738 | tf_op jit(solution)/shard_map/mix_block/pallas_call | solution.py:482
  283.5 23.0 %collective-permute-done.30.refs_2_ = bf16[256,2048]{1,0:T(8,128)(2,1)S(1)} collective-permute-done((bf16[256,2048]{1,0:T(8,128)(2,1)}, bf16[256,2048]{1,0:T(8,128)(2,1)S(1)}, u32[]{:S(2)}, u32[]{:S(2)}) %collective-permute-start.30) | collective-permute-done | bytes 1048608 | tf_op jit(solution)/shard_map/ppermute | solution.py:1006
  317.6 22.5 %collective-permute-done.32.refs_6_ = bf16[256,2048]{1,0:T(8,128)(2,1)S(1)} collective-permute-done((bf16[256,2048]{1,0:T(8,128)(2,1)S(1)}, bf16[256,2048]{1,0:T(8,128)(2,1)S(1)}, u32[]{:S(2)}, u32[]{:S(2)}) %collective-permute-start.32) | collective-permute-done | bytes 1048608 | tf_op jit(solution)/shard_map/ppermute | solution.py:1006
  352.6 21.0 %collective-permute-done.42.f0.refs_16_ = bf16[1296,512]{1,0:T(8,128)(2,1)S(1)} collective-permute-done((bf16[1296,512]{1,0:T(8,128)(2,1)S(1)}, bf16[1296,512]{1,0:T(8,128)(2,1)S(1)}, u32[]{:S(2)}, u32[]{:S(2)}) %collective-permute-start.42) | collective-permute-done | bytes 1327136 | tf_op jit(solution)/shard_map/ppermute | solution.py:1006
  442.1 13.1 %sum_blocks.10 = bf16[512,2048]{1,0:T(8,128)(2,1)} custom-call(bf16[1296,512]{1,0:T(8,128)(2,1)S(1)} %copy-done.34, bf16[1296,512]{1,0:T(8,128)(2,1)S(1)} %copy-done.29, bf16[1296,512]{1,0:T(8,128)(2,1)S(1)} %ffn_block.12.refs_2_.a1, bf16[1296,512]{1,0:T(8,128)(2,1)S(1)} %ffn_block.13.refs_3_.a1, bf16[1296,512]{1,0:T(8,128)(2,1)} %copy-done.10, ...), custom_call_target="tpu_custom_call" | custom-call | flops 2174327296 | bytes 6566708 | tf_op jit(solution)/shard_map/sum_blocks/pallas_call | solution.py:648
  496.8 13.7 %sum_blocks.11.partial = f32[512,2048]{1,0:T(8,128)} custom-call(bf16[1296,512]{1,0:T(8,128)(2,1)S(1)} %copy-done.24, bf16[1296,512]{1,0:T(8,128)(2,1)S(1)} %copy-done.27, bf16[1296,512]{1,0:T(8,128)(2,1)S(1)} %copy-done.32, bf16[1296,512]{1,0:T(8,128)(2,1)S(1)} %ffn_block.15.refs_3_.a0, bf16[1296,512]{1,0:T(8,128)(2,1)} %copy-done.10, ...), custom_call_target="tpu_custom_call" | custom-call | flops 2174327296 | bytes 6566708 | tf_op jit(solution)/shard_map/sum_blocks/pallas_call | solution.py:648
  586.5 12.7 %mix_back_block.4.grad_ref.refs_1_ = bf16[1376,1024]{1,0:T(8,128)(2,1)} custom-call(s32[2]{0:T(128)S(1)} %pad_add_fusion.4.spots_ref, bf16[512,2048]{1,0:T(8,128)(2,1)} %copy-done, bf16[512,2048]{1,0:T(8,128)(2,1)} %collective-permute-done.51.s1, bf16[1824,512]{1,0:T(8,128)(2,1)} %collective-permute-done.3.m0.refs_8_, ...), custom_call_target="tpu_custom_call" | custom-call | flops 1570347392 | bytes 5033165 | tf_op jit(solution)/shard_map/mix_back_block/pallas_call | solution.py:554
  599.3 13.5 %mix_grad_block.4 = (bf16[1808,512]{1,0:T(8,128)(2,1)S(1)}, bf16[1808,512]{1,0:T(8,128)(2,1)S(1)}, bf16[1808,512]{1,0:T(8,128)(2,1)}, bf16[1808,512]{1,0:T(8,128)(2,1)}) custom-call(bf16[512,2048]{1,0:T(8,128)(2,1)} %copy-done, bf16[512,2048]{1,0:T(8,128)(2,1)} %collective-permute-done.51.s1, bf16[1024,2048]{1,0:T(8,128)(2,1)} %get-tuple-element.243.x_ref, ...), custom_call_target="tpu_custom_call" | custom-call | flops 2274990592 | bytes 6291457 | tf_op jit(solution)/shard_map/mix_grad_block/pallas_call | solution.py:594
  655.6 13.3 %mix_grad_block.5 = (bf16[1808,512]{1,0:T(8,128)(2,1)S(1)}, bf16[1808,512]{1,0:T(8,128)(2,1)S(1)}, bf16[1808,512]{1,0:T(8,128)(2,1)}, bf16[1808,512]{1,0:T(8,128)(2,1)}) custom-call(bf16[512,2048]{1,0:T(8,128)(2,1)} %copy-done, bf16[512,2048]{1,0:T(8,128)(2,1)} %collective-permute-done.51.s1, bf16[1024,2048]{1,0:T(8,128)(2,1)} %get-tuple-element.243.x_ref, ...), custom_call_target="tpu_custom_call" | custom-call | flops 2274990592 | bytes 6291457 | tf_op jit(solution)/shard_map/mix_grad_block/pallas_call | solution.py:594
  707.7 12.8 %mix_back_block.6.grad_ref.refs_3_ = bf16[1376,1024]{1,0:T(8,128)(2,1)} custom-call(s32[2]{0:T(128)S(1)} %pad_add_fusion.2.spots_ref, bf16[512,2048]{1,0:T(8,128)(2,1)} %copy-done, bf16[512,2048]{1,0:T(8,128)(2,1)} %collective-permute-done.51.s1, bf16[1824,512]{1,0:T(8,128)(2,1)} %collective-permute-done.17.m0.refs_16_, ...), custom_call_target="tpu_custom_call" | custom-call | flops 1570347392 | bytes 5033165 | tf_op jit(solution)/shard_map/mix_back_block/pallas_call | solution.py:554
  732.8 13.5 %mix_grad_block.6 = (bf16[1808,512]{1,0:T(8,128)(2,1)S(1)}, bf16[1808,512]{1,0:T(8,128)(2,1)S(1)}, bf16[1808,512]{1,0:T(8,128)(2,1)}, bf16[1808,512]{1,0:T(8,128)(2,1)}) custom-call(bf16[512,2048]{1,0:T(8,128)(2,1)} %copy-done, bf16[512,2048]{1,0:T(8,128)(2,1)} %collective-permute-done.51.s1, bf16[1024,2048]{1,0:T(8,128)(2,1)} %get-tuple-element.243.x_ref, ...), custom_call_target="tpu_custom_call" | custom-call | flops 2274990592 | bytes 6291457 | tf_op jit(solution)/shard_map/mix_grad_block/pallas_call | solution.py:594
  755.0 18.0 %sum_blocks.14 = bf16[512,2048]{1,0:T(8,128)(2,1)} custom-call(bf16[1376,1024]{1,0:T(8,128)(2,1)} %mix_back_block.7.refs_0_.grad_ref, bf16[1376,1024]{1,0:T(8,128)(2,1)} %mix_back_block.4.grad_ref.refs_1_, bf16[1376,1024]{1,0:T(8,128)(2,1)} %mix_back_block.5.grad_ref.refs_2_, bf16[1376,1024]{1,0:T(8,128)(2,1)} %mix_back_block.6.grad_ref.refs_3_, ...), custom_call_target="tpu_custom_call" | custom-call | flops 3462817280 | bytes 9712436 | tf_op jit(solution)/shard_map/sum_blocks/pallas_call | solution.py:648
  773.1 13.8 %mix_grad_block.7 = (bf16[1808,512]{1,0:T(8,128)(2,1)S(1)}, bf16[1808,512]{1,0:T(8,128)(2,1)S(1)}, bf16[1808,512]{1,0:T(8,128)(2,1)}, bf16[1808,512]{1,0:T(8,128)(2,1)}) custom-call(bf16[512,2048]{1,0:T(8,128)(2,1)} %copy-done, bf16[512,2048]{1,0:T(8,128)(2,1)} %collective-permute-done.51.s1, bf16[1024,2048]{1,0:T(8,128)(2,1)} %get-tuple-element.243.x_ref, ...), custom_call_target="tpu_custom_call" | custom-call | flops 2274990592 | bytes 6291457 | tf_op jit(solution)/shard_map/mix_grad_block/pallas_call | solution.py:594
  807.4 18.8 %sum_blocks.15.partial = f32[512,2048]{1,0:T(8,128)} custom-call(bf16[1376,1024]{1,0:T(8,128)(2,1)} %mix_back_block.7.refs_0_.grad_ref, bf16[1376,1024]{1,0:T(8,128)(2,1)} %mix_back_block.4.grad_ref.refs_1_, bf16[1376,1024]{1,0:T(8,128)(2,1)} %mix_back_block.5.grad_ref.refs_2_, bf16[1376,1024]{1,0:T(8,128)(2,1)} %mix_back_block.6.grad_ref.refs_3_, ...), custom_call_target="tpu_custom_call" | custom-call | flops 3462817280 | bytes 9712436 | tf_op jit(solution)/shard_map/sum_blocks/pallas_call | solution.py:648
  829.8 15.1 %collective-permute-done.83 = bf16[1808,512]{1,0:T(8,128)(2,1)} collective-permute-done((bf16[1808,512]{1,0:T(8,128)(2,1)}, bf16[1808,512]{1,0:T(8,128)(2,1)}, u32[]{:S(2)}, u32[]{:S(2)}) %collective-permute-start.83) | collective-permute-done | bytes 1851424 | tf_op jit(solution)/shard_map/ppermute | solution.py:1006
  867.1 23.0 %collective-permute-done.92 = f32[2,2048]{1,0:T(2,128)S(1)} collective-permute-done((f32[2,2048]{1,0:T(2,128)S(1)}, f32[2,2048]{1,0:T(2,128)S(1)}, u32[]{:S(2)}, u32[]{:S(2)}) %collective-permute-start.92) | collective-permute-done | bytes 16416 | tf_op jit(solution)/shard_map/ppermute | solution.py:1194
  927.3 24.1 %collective-permute-done.82.got = bf16[1296,256]{1,0:T(8,128)(2,1)S(1)} collective-permute-done((bf16[1296,256]{1,0:T(8,128)(2,1)}, bf16[1296,256]{1,0:T(8,128)(2,1)S(1)}, u32[]{:S(2)}, u32[]{:S(2)}) %collective-permute-start.82) | collective-permute-done | bytes 663584 | tf_op jit(solution)/shard_map/ppermute | solution.py:1006
  (557 shorter events, 544.5 us)
Async XLA Ops:
  120.8 47.6 %collective-permute-start.14 = (bf16[1824,512]{1,0:T(8,128)(2,1)S(1)}, bf16[1824,512]{1,0:T(8,128)(2,1)S(1)}, u32[]{:S(2)}, u32[]{:S(2)}) collective-permute-start(bf16[1824,512]{1,0:T(8,128)(2,1)S(1)} %join.2.m0.refs_4_), channel_id=1, source_target_pairs={{0,4},{4,0},{1,5},{5,1},{2,6},{6,2},{3,7},{7,3},{8,12},{12,8},{9,1... | collective-permute-start | bytes 5603336 | tf_op jit(solution)/shard_map/ppermute | solution.py:1080
  254.2 52.3 %collective-permute-start.33 = (bf16[1296,512]{1,0:T(8,128)(2,1)S(1)}, bf16[1296,512]{1,0:T(8,128)(2,1)}, u32[]{:S(2)}, u32[]{:S(2)}) collective-permute-start(bf16[1296,512]{1,0:T(8,128)(2,1)S(1)} %join.3.f0.refs_4_), channel_id=1, source_target_pairs={{0,1},{1,2},{2,3},{3,0},{4,5},{5,6},{6,7},{7,4},{8,9},{9,10},{10,1... | collective-permute-start | bytes 3981320 | tf_op jit(solution)/shard_map/ppermute | solution.py:1006
  254.2 52.3 %collective-permute-start.35 = (bf16[1296,512]{1,0:T(8,128)(2,1)S(1)}, bf16[1296,512]{1,0:T(8,128)(2,1)}, u32[]{:S(2)}, u32[]{:S(2)}) collective-permute-start(bf16[1296,512]{1,0:T(8,128)(2,1)S(1)} %join.3.f0.refs_4_), channel_id=1, source_target_pairs={{0,16},{16,0},{1,17},{17,1},{2,18},{18,2},{3,19},{19,3},{4,20},{20... | collective-permute-start | bytes 3981320 | tf_op jit(solution)/shard_map/ppermute | solution.py:1006
  255.7 50.8 %collective-permute-start.30 = (bf16[256,2048]{1,0:T(8,128)(2,1)}, bf16[256,2048]{1,0:T(8,128)(2,1)S(1)}, u32[]{:S(2)}, u32[]{:S(2)}) collective-permute-start(bf16[256,2048]{1,0:T(8,128)(2,1)} %copy-done.121), channel_id=1, source_target_pairs={{2,0},{0,2},{7,5},{5,7},{11,9},{9,11},{14,12},{12,14},{18,16},{16,... | collective-permute-start | bytes 3145736 | tf_op jit(solution)/shard_map/ppermute | solution.py:1006
  257.9 49.8 %collective-permute-start.31 = (bf16[256,2048]{1,0:T(8,128)(2,1)}, bf16[256,2048]{1,0:T(8,128)(2,1)S(1)}, u32[]{:S(2)}, u32[]{:S(2)}) collective-permute-start(bf16[256,2048]{1,0:T(8,128)(2,1)} %collective-permute-done.25.refs_3_), channel_id=1, source_target_pairs={{0,8},{9,1},{2,10},{11,3},{12,4},{5,13},{14,6},{7,15},{16,24},{25,... | collective-permute-start | bytes 3145736 | tf_op jit(solution)/shard_map/ppermute | solution.py:1006
  283.4 56.7 %collective-permute-start.29 = (bf16[512,2048]{1,0:T(8,128)(2,1)}, bf16[512,2048]{1,0:T(8,128)(2,1)S(1)}, u32[]{:S(2)}, u32[]{:S(2)}) collective-permute-start(bf16[512,2048]{1,0:T(8,128)(2,1)} %sum_blocks.8), channel_id=1, source_target_pairs={{0,8},{8,0},{1,9},{9,1},{2,10},{10,2},{3,11},{11,3},{4,12},{12,4},... | collective-permute-start | bytes 6291464 | tf_op jit(solution)/shard_map/ppermute | solution.py:1006
  351.3 52.5 %collective-permute-start.39 = (bf16[512,2048]{1,0:T(8,128)(2,1)S(1)}, bf16[512,2048]{1,0:T(8,128)(2,1)}, u32[]{:S(2)}, u32[]{:S(2)}) collective-permute-start(bf16[512,2048]{1,0:T(8,128)(2,1)S(1)} %get-tuple-element.305.x_ref.x0), channel_id=1, source_target_pairs={{0,8},{8,0},{1,9},{9,1},{2,10},{10,2},{3,11},{11,3},{4,12},{12,4},... | collective-permute-start | bytes 6291464 | tf_op jit(solution)/shard_map/ppermute | solution.py:1006
  455.2 58.0 %collective-permute-start.49 = (bf16[512,2048]{1,0:T(8,128)(2,1)}, bf16[512,2048]{1,0:T(8,128)(2,1)S(1)}, u32[]{:S(2)}, u32[]{:S(2)}) collective-permute-start(bf16[512,2048]{1,0:T(8,128)(2,1)} %sum_blocks.10), channel_id=1, source_target_pairs={{0,8},{8,0},{1,9},{9,1},{2,10},{10,2},{3,11},{11,3},{4,12},{12,4},... | collective-permute-start | bytes 6291464 | tf_op jit(solution)/shard_map/ppermute | solution.py:1006
  496.7 56.0 %collective-permute-start.59 = (bf16[1296,512]{1,0:T(8,128)(2,1)}, bf16[1296,512]{1,0:T(8,128)(2,1)}, u32[]{:S(2)}, u32[]{:S(2)}) collective-permute-start(bf16[1296,512]{1,0:T(8,128)(2,1)} %get-tuple-element.307), channel_id=1, source_target_pairs={{0,4},{4,0},{1,5},{5,1},{2,6},{6,2},{3,7},{7,3},{8,12},{12,8},{9,1... | collective-permute-start | bytes 3981320 | tf_op jit(solution)/shard_map/ppermute | solution.py:1080
  513.3 61.2 %collective-permute-start.56 = (bf16[1296,512]{1,0:T(8,128)(2,1)}, bf16[1296,512]{1,0:T(8,128)(2,1)}, u32[]{:S(2)}, u32[]{:S(2)}) collective-permute-start(bf16[1296,512]{1,0:T(8,128)(2,1)} %add_convert_fusion.16), channel_id=1, source_target_pairs={{0,16},{16,0},{1,17},{17,1},{2,18},{18,2},{3,19},{19,3},{4,20},{20... | collective-permute-start | bytes 3981320 | tf_op jit(solution)/shard_map/ppermute | solution.py:1006
  514.3 64.4 %collective-permute-start.58 = (bf16[1296,512]{1,0:T(8,128)(2,1)}, bf16[1296,512]{1,0:T(8,128)(2,1)}, u32[]{:S(2)}, u32[]{:S(2)}) collective-permute-start(bf16[1296,512]{1,0:T(8,128)(2,1)} %get-tuple-element.330), channel_id=1, source_target_pairs={{0,4},{4,0},{1,5},{5,1},{2,6},{6,2},{3,7},{7,3},{8,12},{12,8},{9,1... | collective-permute-start | bytes 3981320 | tf_op jit(solution)/shard_map/ppermute | solution.py:1080
  524.8 61.2 %collective-permute-start.51 = (bf16[512,2048]{1,0:T(8,128)(2,1)S(1)}, bf16[512,2048]{1,0:T(8,128)(2,1)}, u32[]{:S(2)}, u32[]{:S(2)}) collective-permute-start(bf16[512,2048]{1,0:T(8,128)(2,1)S(1)} %get-tuple-element.319.s0), channel_id=1, source_target_pairs={{0,8},{8,0},{1,9},{9,1},{2,10},{10,2},{3,11},{11,3},{4,12},{12,4},... | collective-permute-start | bytes 6291464 | tf_op jit(solution)/shard_map/ppermute | solution.py:1006
  574.4 47.9 %collective-permute-start.50 = (bf16[512,2048]{1,0:T(8,128)(2,1)}, bf16[512,2048]{1,0:T(8,128)(2,1)}, u32[]{:S(2)}, u32[]{:S(2)}) collective-permute-start(bf16[512,2048]{1,0:T(8,128)(2,1)} %sum_blocks.12), channel_id=1, source_target_pairs={{0,8},{8,0},{1,9},{9,1},{2,10},{10,2},{3,11},{11,3},{4,12},{12,4},... | collective-permute-start | bytes 6291464 | tf_op jit(solution)/shard_map/ppermute | solution.py:1006
  586.0 68.8 %collective-permute-start.66 = (bf16[1296,512]{1,0:T(8,128)(2,1)S(1)}, bf16[1296,512]{1,0:T(8,128)(2,1)}, u32[]{:S(2)}, u32[]{:S(2)}) collective-permute-start(bf16[1296,512]{1,0:T(8,128)(2,1)S(1)} %copy-done.119), channel_id=1, source_target_pairs={{0,4},{4,0},{1,5},{5,1},{2,6},{6,2},{3,7},{7,3},{8,12},{12,8},{9,1... | collective-permute-start | bytes 3981320 | tf_op jit(solution)/shard_map/ppermute | solution.py:1080
  612.8 56.2 %collective-permute-start.72 = (bf16[1808,512]{1,0:T(8,128)(2,1)}, bf16[1808,512]{1,0:T(8,128)(2,1)}, u32[]{:S(2)}, u32[]{:S(2)}) collective-permute-start(bf16[1808,512]{1,0:T(8,128)(2,1)} %get-tuple-element.340), channel_id=1, source_target_pairs={{0,4},{4,0},{1,5},{5,1},{2,6},{6,2},{3,7},{7,3},{8,12},{12,8},{9,1... | collective-permute-start | bytes 5554184 | tf_op jit(solution)/shard_map/ppermute | solution.py:1080
  688.7 58.8 %collective-permute-start.74 = (bf16[1808,512]{1,0:T(8,128)(2,1)}, bf16[1808,512]{1,0:T(8,128)(2,1)}, u32[]{:S(2)}, u32[]{:S(2)}) collective-permute-start(bf16[1808,512]{1,0:T(8,128)(2,1)} %add_convert_fusion.8), channel_id=1, source_target_pairs={{0,16},{16,0},{1,17},{17,1},{2,18},{18,2},{3,19},{19,3},{4,20},{20... | collective-permute-start | bytes 5554184 | tf_op jit(solution)/shard_map/ppermute | solution.py:1006
  690.1 61.7 %collective-permute-start.76 = (bf16[1808,512]{1,0:T(8,128)(2,1)}, bf16[1808,512]{1,0:T(8,128)(2,1)}, u32[]{:S(2)}, u32[]{:S(2)}) collective-permute-start(bf16[1808,512]{1,0:T(8,128)(2,1)} %get-tuple-element.381), channel_id=1, source_target_pairs={{0,4},{4,0},{1,5},{5,1},{2,6},{6,2},{3,7},{7,3},{8,12},{12,8},{9,1... | collective-permute-start | bytes 5554184 | tf_op jit(solution)/shard_map/ppermute | solution.py:1080
  698.9 52.4 %collective-permute-start.69 = (bf16[256,2048]{1,0:T(8,128)(2,1)}, bf16[256,2048]{1,0:T(8,128)(2,1)}, u32[]{:S(2)}, u32[]{:S(2)}) collective-permute-start(bf16[256,2048]{1,0:T(8,128)(2,1)} %get-tuple-element.356), channel_id=1, source_target_pairs={{0,1},{2,3},{5,6},{7,4},{9,10},{11,8},{12,13},{14,15},{16,17},{18,... | collective-permute-start | bytes 3145736 | tf_op jit(solution)/shard_map/ppermute | solution.py:1006
  701.7 50.1 %collective-permute-start.70 = (bf16[256,2048]{1,0:T(8,128)(2,1)}, bf16[256,2048]{1,0:T(8,128)(2,1)}, u32[]{:S(2)}, u32[]{:S(2)}) collective-permute-start(bf16[256,2048]{1,0:T(8,128)(2,1)} %get-tuple-element.358), channel_id=1, source_target_pairs={{0,2},{2,0},{5,7},{7,5},{9,11},{11,9},{12,14},{14,12},{16,18},{18,... | collective-permute-start | bytes 3145736 | tf_op jit(solution)/shard_map/ppermute | solution.py:1006
  803.1 46.9 %collective-permute-start.79 = (bf16[512,2048]{1,0:T(8,128)(2,1)}, bf16[512,2048]{1,0:T(8,128)(2,1)}, u32[]{:S(2)}, u32[]{:S(2)}) collective-permute-start(bf16[512,2048]{1,0:T(8,128)(2,1)} %sum_blocks.14), channel_id=1, source_target_pairs={{0,8},{8,0},{1,9},{9,1},{2,10},{10,2},{3,11},{11,3},{4,12},{12,4},... | collective-permute-start | bytes 6291464 | tf_op jit(solution)/shard_map/ppermute | solution.py:1006
  849.4 54.7 %collective-permute-start.87 = (bf16[1808,512]{1,0:T(8,128)(2,1)}, bf16[1808,512]{1,0:T(8,128)(2,1)}, u32[]{:S(2)}, u32[]{:S(2)}) collective-permute-start(bf16[1808,512]{1,0:T(8,128)(2,1)} %add_convert_fusion.3), channel_id=1, source_target_pairs={{0,1},{1,2},{2,3},{3,0},{4,5},{5,6},{6,7},{7,4},{8,9},{9,10},{10,1... | collective-permute-start | bytes 5554184 | tf_op jit(solution)/shard_map/ppermute | solution.py:1006
  849.4 60.9 %collective-permute-start.90 = (bf16[1808,512]{1,0:T(8,128)(2,1)}, bf16[1808,512]{1,0:T(8,128)(2,1)}, u32[]{:S(2)}, u32[]{:S(2)}) collective-permute-start(bf16[1808,512]{1,0:T(8,128)(2,1)} %add_convert_fusion.2), channel_id=1, source_target_pairs={{0,16},{16,0},{1,17},{17,1},{2,18},{18,2},{3,19},{19,3},{4,20},{20... | collective-permute-start | bytes 5554184 | tf_op jit(solution)/shard_map/ppermute | solution.py:1006
  904.1 52.9 %collective-permute-start.100 = (bf16[256,2048]{1,0:T(8,128)(2,1)}, bf16[256,2048]{1,0:T(8,128)(2,1)}, u32[]{:S(2)}, u32[]{:S(2)}) collective-permute-start(bf16[256,2048]{1,0:T(8,128)(2,1)} %get-tuple-element.417), channel_id=1, source_target_pairs={{0,3},{2,1},{5,4},{7,6},{9,8},{11,10},{12,15},{14,13},{16,19},{18,... | collective-permute-start | bytes 3145736 | tf_op jit(solution)/shard_map/ppermute | solution.py:1006
  910.2 46.8 %collective-permute-start.99 = (bf16[256,2048]{1,0:T(8,128)(2,1)}, bf16[256,2048]{1,0:T(8,128)(2,1)}, u32[]{:S(2)}, u32[]{:S(2)}) collective-permute-start(bf16[256,2048]{1,0:T(8,128)(2,1)} %get-tuple-element.415), channel_id=1, source_target_pairs={{0,2},{2,0},{5,7},{7,5},{9,11},{11,9},{12,14},{14,12},{16,18},{18,... | collective-permute-start | bytes 3145736 | tf_op jit(solution)/shard_map/ppermute | solution.py:1006
  (219 other events, 4015.8 us)
